TPU v7x, 32 devices: a whole 2x2x4 slice. The times are simulated.
32 devices in a mesh: ctx: 8 (over z, x), tp: 4 (over y, core).
Axes of the slice: x: 2, y: 2, z: 4, core: 2. Of those that a mesh axis runs over, the one named last changes fastest.
Arguments:
- tokens: bfloat16 [6144, 4096], P('ctx'), may hold values from -6 to 6
- qkv_weight: bfloat16 [3, 4096, 4096], P(None, 'ctx', 'tp'), may hold values from -0.09375 to 0.09375
- short_filter: float32 [3, 7, 4096], P(None, None, 'tp'), may hold values from -2.4 to 2.4
- long_filter: float32 [256, 128], P('tp'), may hold values from -0.9 to 0.9
- decay_rate: float32 [256], P('tp'), may hold values from 0.004 to 0.2
- skip_gain: float32 [4096], P('tp'), may hold values from -3 to 3
- out_weight: bfloat16 [4096, 4096], P('tp', 'ctx'), may hold values from -0.09375 to 0.09375
Outputs:
- block_out: bfloat16 [6144, 4096], P(('ctx', 'tp'))
All inputs are finite; a program needn't handle non-finite values.
Results may differ from a plain program's by a relative error of at most 0.008.
Values may be sent and summed in bfloat16 or wider, within the bound.
No kernel may reach another device: no remote copies, remote signals or barrier semaphores. Data moves between devices by JAX's collectives and lax.ppermute only.
A program may use at most 128 MiB of HBM per device.

v0:
```python
import jax
import jax.numpy as jnp
from jax import lax
from jax.sharding import PartitionSpec as P


def shifted(value, axis, steps):
    count = lax.axis_size(axis)
    first, last = (max(0, -steps), min(count, count - steps))
    return lax.ppermute(value, axis, [(source, source + steps) for source in range(first, last)])


def short_conv(extended, short_filter):
    span = short_filter.shape[1]
    length = extended.shape[2] - (span - 1)
    result = short_filter[:, 0, :, None] * extended[:, :, span - 1 :]
    for offset in range(1, span):
        start = span - 1 - offset
        result = result + short_filter[:, offset, :, None] * extended[:, :, start : start + length]
    return result


def banded(filters):
    tap_count = filters.shape[1]
    row_index = jnp.arange(tap_count)[:, None]
    col_index = jnp.arange(tap_count)[None, :]
    distance = (row_index - col_index) % tap_count
    picker = (distance[None, :, :] == jnp.arange(tap_count)[:, None, None]).astype(jnp.bfloat16)
    full_band = jnp.einsum("gk,kij->gij", filters, picker, preferred_element_type=jnp.float32)
    lower_part = row_index >= col_index
    lower_band = jnp.where(lower_part[None], full_band, 0.0).astype(jnp.bfloat16)
    upper_band = jnp.where(lower_part[None], 0.0, full_band).astype(jnp.bfloat16)
    return (lower_band, upper_band)


def long_mix(features, gated, previous, filters, gain):
    channel_count, length = gated.shape
    tap_count = filters.shape[1]
    group_count = filters.shape[0]
    extended = jnp.concatenate([previous, gated], axis=1)
    blocks = extended.reshape(
        group_count, channel_count // group_count, length // tap_count + 1, tap_count
    )
    lower_band, upper_band = banded(filters)
    current = jnp.einsum(
        "gij,gcbj->gcbi", lower_band, blocks[:, :, 1:], preferred_element_type=jnp.float32
    )
    current = current + jnp.einsum(
        "gij,gcbj->gcbi", upper_band, blocks[:, :, :-1], preferred_element_type=jnp.float32
    )
    filtered = current.reshape(channel_count, length)
    return (features[0] * (filtered + gain[:, None] * gated.astype(jnp.float32))).astype(
        jnp.bfloat16
    )


def per_device(tokens, qkv_weight, short_filter, long_filter, decay_rate, skip_gain, out_weight):
    tok_rows = tokens.shape[0]
    local_width = qkv_weight.shape[2]
    tap_count = long_filter.shape[1]
    span = short_filter.shape[1]
    projected = jnp.einsum(
        "tr,src->sct",
        tokens,
        lax.all_gather(qkv_weight, "ctx", axis=1, tiled=True),
        preferred_element_type=jnp.float32,
    )
    qkv = projected.astype(jnp.bfloat16)
    tap_index = jnp.arange(tap_count, dtype=jnp.float32)
    filters = (long_filter * jnp.exp(-decay_rate[:, None] * tap_index[None, :])).astype(
        jnp.bfloat16
    )
    rim = shifted(qkv[:, :, tok_rows - (span - 1) :], "ctx", 1)
    features = short_conv(jnp.concatenate([rim, qkv], axis=2), short_filter)
    gated = (features[1] * features[2]).astype(jnp.bfloat16)
    tail = shifted(gated[:, tok_rows - (tap_count - 1) :], "ctx", 1)
    previous = jnp.concatenate([jnp.zeros((local_width, 1), jnp.bfloat16), tail], axis=1)
    mixed = long_mix(features, gated, previous, filters, skip_gain)
    out_rows = lax.all_gather(out_weight, "ctx", axis=1, tiled=True)
    summed = lax.psum_scatter(
        lax.dot_general(
            mixed, out_rows, (((0,), (0,)), ((), ())), preferred_element_type=jnp.float32
        ),
        "tp",
        scatter_dimension=0,
        tiled=True,
    )
    return summed.astype(jnp.bfloat16)


def solution(mesh):
    in_specs = (
        P("ctx", None),
        P(None, "ctx", "tp"),
        P(None, None, "tp"),
        P("tp", None),
        P("tp"),
        P("tp"),
        P("tp", "ctx"),
    )
    out_specs = P(("ctx", "tp"), None)
    return jax.shard_map(
        per_device, mesh=mesh, in_specs=in_specs, out_specs=out_specs, check_vma=False
    )
```

profile of v0, /device:TPU:17, one launch (start us, length us, event | category | flops | bytes accessed | tf_op | source)
XLA Modules:
  0.0 740.9 jit_solution(16689934915824206881)
XLA Ops:
  6.5 0.7 all-gather.3.cloned.1.call-update
  7.3 0.7 all-gather.5.cloned.1.call-update
  8.1 1.5 fusion.38
  9.7 481.0 %all-gather.3.cloned.1.call-done = bf16[3,4096,1024]{2,1,0:T(8,128)(2,1)} async-done(((bf16[3,512,1024]{2,1,0:T(8,128)(2,1)}), bf16[3,4096,1024]{2,1,0:T(8,128)(2,1)}) %all-gather.3.cloned.1.call-update) | async-done | bytes 25165840 | tf_op jit(solution)/shard_map/all_gather | solution.py:65
  490.6 25.0 %fusion.12 = bf16[3,1024,768]{1,2,0:T(8,128)(2,1)S(1)} fusion(bf16[3,4096,1024]{2,1,0:T(8,128)(2,1)} %all-gather.3.cloned.1.call-done, bf16[768,4096]{1,0:T(8,128)(2,1)} %param.7), kind=kOutput, calls=%fused_computation.28 | convolution fusion | flops 19329712128 | bytes 36175872 | tf_op jit(solution)/shard_map/tr,src->sct/dot_general | solution.py:62
  515.6 2.0 collective-permute-start
  517.7 6.5 collective-permute-done
  524.2 8.5 %multiply_add_fusion = f32[3,1024,768]{1,2,0:T(8,128)S(1)} fusion(bf16[3,1024,768]{1,2,0:T(8,128)(2,1)S(1)} %fusion.12, bf16[3,1024,6]{1,2,0:T(8,128)(2,1)S(1)} %collective-permute-done, f32[3,1024]{1,0:T(4,128)S(1)} %get-tuple-element.16, f32[3,1024]{1,0:T(4,128)S(1)} %get-tuple-element.17, f32[3,1024]{1,0:T(4,128)S(1)} %get-tuple-element.18, ...), kind=kLoop, calls=%fused_computation.5 | loop fusion | flops 89653248 | bytes 14278656 | tf_op jit(solution)/shard_map/add | solution.py:19
  533.4 1.9 collective-permute-start.1
  535.3 4.5 fusion.15
  539.8 5.6 collective-permute-done.1
  545.8 2.7 copy.13
  548.5 3.7 reshape.53
  552.2 0.9 fusion.37
  553.1 0.7 copy-done.3
  553.8 2.3 fusion.17
  556.1 2.3 fusion.21
  558.4 1.4 copy.18
  559.9 0.8 copy.54
  560.6 2.4 copy.19
  563.1 55.5 %all-gather.5.cloned.1.call-done = bf16[1024,4096]{1,0:T(8,128)(2,1)} async-done(((bf16[1024,512]{1,0:T(8,128)(2,1)}), bf16[1024,4096]{1,0:T(8,128)(2,1)}) %all-gather.5.cloned.1.call-update) | async-done | bytes 8388624 | tf_op jit(solution)/shard_map/all_gather | solution.py:79
  618.5 13.9 %fusion.24 = f32[768,4096]{1,0:T(8,128)} fusion(bf16[1024,4096]{1,0:T(8,128)(2,1)} %all-gather.5.cloned.1.call-done, f32[3,1024,768]{1,2,0:T(8,128)} %copy-done, f32[1024,768]{0,1:T(8,128)} %copy.19, bf16[1024,768]{0,1:T(8,128)(2,1)} %copy-done.1, f32[1024]{0:T(1024)S(1)} %copy-done.5), kind=kOutput, calls=%fused_computation.37 | convolution fusion | flops 6446383104 | bytes 28839936 | tf_op jit(solution)/shard_map/dot_general | solution.py:81
  632.5 98.7 %reduce-scatter.2.cloned.1.call-done = f32[192,4096]{1,0:T(8,128)} async-done(((f32[768,4096]{1,0:T(8,128)}), f32[192,4096]{1,0:T(8,128)}) %reduce-scatter.2.cloned.1.call-update) | async-done | bytes 3145744 | tf_op jit(solution)/shard_map/reduce_scatter | solution.py:80
  731.2 3.2 convert_element_type.64
  (29 shorter events, 1.2 us)
Async XLA Ops:
  6.5 484.1 %all-gather.3.cloned.1.call-start = ((), (), s32[]{:S(2)}) async-start(), calls=%async_computation.1 | async-start | bytes 28311552 | tf_op jit(solution)/shard_map/all_gather | solution.py:65
  7.3 611.2 %all-gather.5.cloned.1.call-start = ((), (), s32[]{:S(2)}) async-start(), calls=%async_computation.2 | async-start | bytes 9437184 | tf_op jit(solution)/shard_map/all_gather | solution.py:79
  8.0 723.2 %reduce-scatter.2.cloned.1.call-start = ((), (), s32[]{:S(2)}) async-start(), calls=%async_computation.3 | async-start | bytes 15728640 | tf_op jit(solution)/shard_map/reduce_scatter | solution.py:80
  9.6 508.0 %copy-start.6 = (f32[64]{0:T(128)S(1)}, f32[64]{0:T(128)}, u32[]{:S(2)}) copy-start(f32[64]{0:T(128)} %param.11) | copy-start | bytes 772
  515.6 8.6 %collective-permute-start = (bf16[3,1024,6]{1,2,0:T(8,128)(2,1)S(1)}, bf16[3,1024,6]{1,2,0:T(8,128)(2,1)S(1)}, u32[]{:S(2)}, u32[]{:S(2)}) collective-permute-start(bf16[3,1024,6]{1,2,0:T(8,128)(2,1)S(1)} %slice.80), channel_id=1, source_target_pairs={{0,4},{4,8},{8,12},{12,16},{16,20},{20,24},{24,28},{1,5},{5,9},{9,... | collective-permute-start | bytes 110600 | tf_op jit(solution)/shard_map/ppermute | solution.py:10
  532.7 7.1 copy-start
  532.7 2.6 copy-start.4
  533.3 12.1 %copy-start.1 = (bf16[1024,768]{0,1:T(8,128)(2,1)}, bf16[1024,768]{0,1:T(8,128)(2,1)S(1)}, u32[]{:S(2)}) copy-start(bf16[1024,768]{0,1:T(8,128)(2,1)S(1)} %fusion.26) | copy-start | bytes 4718596
  533.4 12.0 %collective-permute-start.1 = (bf16[1024,127]{0,1:T(8,128)(2,1)S(1)}, bf16[1024,127]{0,1:T(8,128)(2,1)S(1)}, u32[]{:S(2)}, u32[]{:S(2)}) collective-permute-start(bf16[1024,127]{0,1:T(8,128)(2,1)S(1)} %slice.94), channel_id=1, source_target_pairs={{0,4},{4,8},{8,12},{12,16},{16,20},{20,24},{24,28},{1,5},{5,9},{9,... | collective-permute-start | bytes 780296 | tf_op jit(solution)/shard_map/ppermute | solution.py:10
  552.2 1.6 copy-start.3
  553.1 3.0 copy-start.2
  560.6 57.9 %copy-start.5 = (f32[1024]{0:T(1024)S(1)}, f32[1024]{0:T(1024)}, u32[]{:S(2)}) copy-start(f32[1024]{0:T(1024)} %param.12) | copy-start | bytes 12292
Sparse Core Ops, SparseCore 0:
  8.9 481.6 all-gather.2
  492.7 125.7 all-gather.4
  632.6 98.5 reduce-scatter.1
where the time goes:
time: 743 us; the launch traced here: 741 us
  waiting for transfers between devices  649 us (87%)
  matrix products  48.1 us (6%)
  local copies, waits for them, and re-layouts  14.2 us (2%)
  between operations  13.3 us (2%)
  other arithmetic  12.7 us (2%)
    all_gather x1, waiting for transfers between devices, per_device(): lax.all_gather(qkv_weight, 'ctx', axis=1, tiled=True)  481 us
    reduce_scatter x1, waiting for transfers between devices, per_device(): lax.psum_scatter(lax.dot_general(mixed, out_rows, (((0,), (0,)), ((), ())...  98.7 us
    all_gather x1, waiting for transfers between devices, per_device(): out_rows = lax.all_gather(out_weight, 'ctx', axis=1, tiled=True)  55.5 us
    dot_general x1, matrix products, per_device(): jnp.einsum('tr,src->sct', tokens, lax.all_gather(qkv_weight, 'ctx', axis=...  25 us
  transfers between devices with their start and end apart: 5, of which 5 were waited for; matrix products, arithmetic and copies ran while one was open for 8% of the time, Pallas kernels for 0%

commit v1 on v0

v1 whole, which is shorter than its diff:
```python
import functools

import jax
import jax.numpy as jnp
from jax import lax
from jax.experimental import pallas as pl
from jax.experimental.pallas import tpu as pltpu
from jax.sharding import PartitionSpec as P

AXES = ("ctx", "tp")
BF16, F32 = jnp.bfloat16, jnp.float32
VMEM_LIMIT = 56 << 20
IN_FLIGHT = 2


class Places:
    def __init__(self, ctx, tp):
        self.ctx, self.tp = ctx, tp
        self.nx = 1 << ((ctx.bit_length() - 1) // 2)
        self.ny = tp // 2

    def device(self, v, w):
        core, zl = (v // self.nx) % 2, w % 2
        return (v + (zl - core) * self.nx) * self.tp + w + core - zl

    def here(self):
        i, j = lax.axis_index("ctx"), lax.axis_index("tp")
        core, zl = j % 2, (i // self.nx) % 2
        return i + (core - zl) * self.nx, j + zl - core

    def at_home(self, v, w):
        return (v // self.nx) % 2 == w % 2

    def deliver(self, value, mask=0):
        pairs = []
        for i in range(self.ctx):
            for j in range(self.tp):
                source, target = i * self.tp + j, self.device(i ^ mask, j)
                if source != target:
                    pairs.append((source, target))
        return lax.ppermute(value, AXES, pairs)

    def send(self, value, target):
        pairs = []
        for v in range(self.ctx):
            for w in range(self.tp):
                to = target(v, w)
                if to is not None:
                    pairs.append((self.device(v, w), self.device(*to)))
        return lax.ppermute(value, AXES, pairs)

    def spread_masks(self):
        far = [step * 2 * self.nx for step in range(self.ctx // (2 * self.nx))]
        groups = [[m ^ step for m in far] for step in range(self.nx)]
        return groups + [[m ^ self.nx for m in group] for group in groups]


def after(value, done):
    return lax.optimization_barrier((value, done))[0] if done is not None else value


def gather(places, home, shard, line):
    far = []
    for step in range(1, places.ctx // (2 * places.nx)):
        far.append(places.deliver(after(shard, line[-IN_FLIGHT]), step * 2 * places.nx))
        line.append(far[-1])
    near = places.deliver(after(shard, line[-IN_FLIGHT]))
    held = jnp.stack([jnp.where(home, shard, near)] + far)
    stacks = [held]
    for step in range(1, places.nx):
        stacks.append(places.send(held, lambda v, w, m=step: (v ^ m, w)))
    return stacks + [places.send(stack, lambda v, w: (v ^ places.nx, w)) for stack in stacks]


def prepare_kernel(per_part, order, flags, own, *refs):
    parts, out = refs[:-1], refs[-1]
    part = order[pl.program_id(0)] // per_part

    @pl.when(flags[0] == 1)
    def _():
        out[...] = own[...].T

    for step, ref in enumerate(parts):

        @pl.when((flags[0] == 0) & (part == flags[1] ^ step))
        def _():
            out[...] = ref[...].T


def prepare(order, flags, own, parts, depth):
    rows, features = own.shape
    count = features // depth
    per_part = count // len(parts)
    return pl.pallas_call(
        functools.partial(prepare_kernel, per_part),
        out_shape=jax.ShapeDtypeStruct((features, rows), BF16),
        grid_spec=pltpu.PrefetchScalarGridSpec(
            num_scalar_prefetch=2,
            grid=(count,),
            in_specs=[pl.BlockSpec((rows, depth), lambda i, o, f: (0, o[i]))]
            + [pl.BlockSpec((rows, depth), lambda i, o, f: (0, o[i] % per_part))] * len(parts),
            out_specs=pl.BlockSpec((depth, rows), lambda i, o, f: (i, 0)),
        ),
        compiler_params=pltpu.CompilerParams(vmem_limit_bytes=VMEM_LIMIT),
        cost_estimate=pl.CostEstimate(
            flops=0, bytes_accessed=6 * rows * features, transcendentals=0
        ),
    )(order, flags, own, *parts)


def project_kernel(tokens, *refs):
    stacks, out = refs[:-1], refs[-1]
    pieces = [stack[index] for stack in stacks for index in range(stack.shape[0])]
    out[...] = jnp.dot(
        jnp.concatenate(pieces, axis=1), tokens[...], preferred_element_type=F32
    ).astype(out.dtype)


def project(tokens, stacks):
    features, rows = tokens.shape
    count, width, depth = stacks[0].shape
    tile = min(256, width)
    return pl.pallas_call(
        project_kernel,
        out_shape=jax.ShapeDtypeStruct((width, rows), BF16),
        grid=(width // tile,),
        in_specs=[pl.BlockSpec((features, rows), lambda i: (0, 0))]
        + [pl.BlockSpec((count, tile, depth), lambda i: (0, i, 0))] * len(stacks),
        out_specs=pl.BlockSpec((tile, rows), lambda i: (i, 0)),
        compiler_params=pltpu.CompilerParams(vmem_limit_bytes=VMEM_LIMIT),
        cost_estimate=pl.CostEstimate(
            flops=2 * width * rows * features,
            bytes_accessed=2 * ((width + rows) * features + width * rows),
            transcendentals=0,
        ),
    )(tokens, *stacks)


def featurize(rim, value, coefficients, first, span):
    wide = jnp.concatenate([rim, value], axis=1).astype(F32)
    total = coefficients[:, first : first + 1] * wide
    for offset in range(1, span):
        total = total + coefficients[:, first + offset : first + offset + 1] * pltpu.roll(
            wide, offset, 1
        )
    return total[:, rim.shape[1] :]


def filter_kernel(span, k, v, k_rim, v_rim, before, coefficients, bands, out):
    coef = coefficients[...]
    first = featurize(k_rim[...], k[...], coef, span, span)
    second = featurize(v_rim[...], v[...], coef, 2 * span, span)
    gated = (first * second).astype(BF16)
    wide = jnp.concatenate([before[...], gated], axis=1)
    groups, reach, taps = bands.shape
    size = wide.shape[0] // groups
    blocks = gated.shape[1] // taps
    for group in range(groups):
        rows = slice(group * size, (group + 1) * size)
        windows = jnp.concatenate(
            [wide[rows, block * taps : block * taps + reach] for block in range(blocks)], axis=0
        )
        sums = jnp.dot(windows, bands[group], preferred_element_type=F32)
        gain = coef[rows, 3 * span : 3 * span + 1]
        for block in range(blocks):
            lanes = slice(block * taps, (block + 1) * taps)
            out[rows, lanes] = sums[block * size : (block + 1) * size] + gain * gated[
                rows, lanes
            ].astype(F32)


def long_filter_part(span, k, v, k_rim, v_rim, before, coefficients, bands):
    width, rows = k.shape
    groups, reach, taps = bands.shape
    tile = min(128, width)
    tall = lambda size: pl.BlockSpec((tile, size), lambda i: (i, 0))
    return pl.pallas_call(
        functools.partial(filter_kernel, span),
        out_shape=jax.ShapeDtypeStruct((width, rows), F32),
        grid=(width // tile,),
        in_specs=[tall(rows), tall(rows), tall(taps), tall(taps), tall(taps)]
        + [
            tall(coefficients.shape[1]),
            pl.BlockSpec((groups * tile // width, reach, taps), lambda i: (i, 0, 0)),
        ],
        out_specs=tall(rows),
        compiler_params=pltpu.CompilerParams(vmem_limit_bytes=VMEM_LIMIT),
        cost_estimate=pl.CostEstimate(
            flops=2 * width * rows * (reach + 4 * span),
            bytes_accessed=8 * width * rows + 2 * groups * reach * taps,
            transcendentals=0,
        ),
    )(k, v, k_rim, v_rim, before, coefficients, bands)


def mix_kernel(span, q, q_rim, filtered, coefficients, out):
    features = featurize(q_rim[...], q[...], coefficients[...], 0, span)
    out[...] = (features * filtered[...]).T.astype(BF16)


def mix(span, q, q_rim, filtered, coefficients):
    width, rows = q.shape
    tile = min(128, width)
    tall = lambda size: pl.BlockSpec((tile, size), lambda i: (i, 0))
    return pl.pallas_call(
        functools.partial(mix_kernel, span),
        out_shape=jax.ShapeDtypeStruct((rows, width), BF16),
        grid=(width // tile,),
        in_specs=[tall(rows), tall(q_rim.shape[1]), tall(rows), tall(coefficients.shape[1])],
        out_specs=pl.BlockSpec((rows, tile), lambda i: (0, i)),
        compiler_params=pltpu.CompilerParams(vmem_limit_bytes=VMEM_LIMIT),
        cost_estimate=pl.CostEstimate(
            flops=2 * width * rows * span, bytes_accessed=8 * width * rows, transcendentals=0
        ),
    )(q, q_rim, filtered, coefficients)


def output_kernel(count, order, *refs):
    mixed, stacks, out = refs[:count], refs[count:-1], refs[-1]
    left = jnp.concatenate([ref[...] for ref in mixed], axis=1)
    width = stacks[0].shape[2]
    place = 0
    for stack in stacks:
        for index in range(stack.shape[0]):
            start = pl.multiple_of(order[place] * width, width)
            out[:, pl.ds(start, width)] = jnp.dot(
                left, stack[index], preferred_element_type=F32
            ).astype(out.dtype)
            place += 1


def output_sums(order, mixed, stacks):
    rows, part = mixed[0].shape
    count, depth, width = stacks[0].shape
    features = width * count * len(stacks)
    tile = min(256, rows)
    return pl.pallas_call(
        functools.partial(output_kernel, len(mixed)),
        out_shape=jax.ShapeDtypeStruct((rows, features), BF16),
        grid_spec=pltpu.PrefetchScalarGridSpec(
            num_scalar_prefetch=1,
            grid=(rows // tile,),
            in_specs=[pl.BlockSpec((tile, part), lambda i, o: (i, 0))] * len(mixed)
            + [pl.BlockSpec((count, depth, width), lambda i, o: (0, 0, 0))] * len(stacks),
            out_specs=pl.BlockSpec((tile, features), lambda i, o: (i, 0)),
        ),
        compiler_params=pltpu.CompilerParams(vmem_limit_bytes=VMEM_LIMIT),
        cost_estimate=pl.CostEstimate(
            flops=2 * rows * depth * features,
            bytes_accessed=2 * (rows * depth + depth * features + rows * features),
            transcendentals=0,
        ),
    )(order, *mixed, *stacks)


def bands_of(filters):
    taps = filters.shape[1]
    source = jnp.arange(taps)[:, None]
    target = jnp.arange(taps)[None, :]
    distance = (target - source) % taps
    picker = (distance[None] == jnp.arange(taps)[:, None, None]).astype(BF16)
    full = jnp.einsum("gk,kji->gji", filters, picker, preferred_element_type=F32)
    same = target >= source
    before, current = jnp.where(same, 0.0, full), jnp.where(same, full, 0.0)
    return jnp.concatenate([before, current], axis=1).astype(BF16)


def tail_gate(k, v, taps_k, taps_v, reach):
    span = taps_k.shape[0]

    def features(value, taps):
        wide = value[:, value.shape[1] - reach - span + 1 :].astype(F32)
        total = taps[0][:, None] * wide[:, span - 1 :]
        for offset in range(1, span):
            start = span - 1 - offset
            total = total + taps[offset][:, None] * wide[:, start : start + reach]
        return total

    return (features(k, taps_k) * features(v, taps_v)).astype(BF16)


def take(value, part, size):
    return lax.dynamic_slice_in_dim(value, part * size, size)


def sum_over_y(places, sums, y):
    part = sums.shape[0] // places.ny
    total = take(sums, y, part).astype(F32)
    for step in range(1, places.ny):
        other = take(sums, y ^ step, part)
        total = total + places.send(other, lambda a, b, m=2 * step: (a, b ^ m)).astype(F32)
    return total


def sum_over_zl(places, mine, yours, home):
    nx = places.nx
    first = places.send(
        jnp.where(home, yours, mine).astype(BF16),
        lambda a, b: (a ^ nx, b) if places.at_home(a, b) else (a, b ^ 1),
    )
    second = places.send(
        yours.astype(BF16), lambda a, b: None if places.at_home(a, b) else (a ^ nx, b ^ 1)
    )
    return first.astype(F32) + jnp.where(home, mine.astype(F32), second.astype(F32))


def per_device(
    places, tokens, qkv_weight, short_filter, long_filter, decay_rate, skip_gain, out_weight
):
    rows, in_features = tokens.shape
    depth, width = qkv_weight.shape[1:]
    groups, taps = long_filter.shape
    span = short_filter.shape[1]
    ny, nx = places.ny, places.nx
    v, w = places.here()
    y, zl = w // 2, w % 2
    core = (v // nx) % 2
    home = core == zl
    half = width // 2
    chunks = max(1, out_weight.shape[1] // 256)
    chunk = out_weight.shape[1] // chunks
    order = jnp.stack([v ^ m for group in places.spread_masks() for m in group]).astype(jnp.int32)
    flags = jnp.stack([home.astype(jnp.int32), y.astype(jnp.int32)])

    line = [None] * IN_FLIGHT
    pieces = {}
    pieces[1, 0] = gather(places, home, qkv_weight[1, :, :half].T, line)

    share = in_features // ny
    mine = places.deliver(lax.dynamic_slice_in_dim(tokens, y * share, share, 1))
    parts = [mine]
    for step in range(1, ny):
        parts.append(
            places.send(
                mine,
                lambda a, b, m=2 * step: None if places.at_home(a, b) else (a, b ^ m),
            )
        )
    tokens = prepare(order, flags, tokens, parts, depth)

    for s, h in ((2, 0), (1, 1), (2, 1), (0, 0), (0, 1)):
        pieces[s, h] = gather(places, home, qkv_weight[s, :, h * half : (h + 1) * half].T, line)
    outs = [
        gather(places, home, out_weight[:, c * chunk : (c + 1) * chunk], line)
        for c in range(chunks)
    ]

    tap_index = jnp.arange(taps, dtype=F32)
    filters = (long_filter * jnp.exp(-decay_rate[:, None] * tap_index[None, :])).astype(BF16)
    packed = jnp.concatenate(
        [
            short_filter.reshape(3 * span, width),
            skip_gain[None, :],
            filters.astype(F32).reshape(-1, width),
        ]
    )
    packed = jnp.where(home, packed, places.deliver(packed))
    short = packed[: 3 * span].reshape(3, span, width)
    coefficients = jnp.pad(packed[: 3 * span + 1].T, ((0, 0), (0, (-3 * span - 1) % 8)))
    bands = bands_of(packed[3 * span + 1 :].reshape(groups, taps).astype(BF16))

    def forward(a, b):
        return (a + 1, b) if a + 1 < places.ctx else None

    def rim_of(value):
        return jnp.pad(value.T, ((0, 0), (taps - value.shape[0], 0)))

    edge = 8 * -(-(span - 1) // 8)
    mixed = []
    filtered = []
    for h in range(2):
        lanes = slice(h * half, (h + 1) * half)
        k = project(tokens, pieces[1, h])
        u = project(tokens, pieces[2, h])
        tail = tail_gate(k, u, short[1, :, lanes], short[2, :, lanes], taps)
        halo = jnp.concatenate([tail.T, k[:, rows - edge :].T, u[:, rows - edge :].T])
        halo = places.send(halo, forward)
        filtered.append(
            long_filter_part(
                span,
                k,
                u,
                rim_of(halo[taps : taps + edge]),
                rim_of(halo[taps + edge :]),
                halo[:taps].T,
                coefficients[lanes],
                bands[h * groups // 2 : (h + 1) * groups // 2],
            )
        )
    for h in range(2):
        lanes = slice(h * half, (h + 1) * half)
        q = project(tokens, pieces[0, h])
        rim = rim_of(places.send(q[:, rows - edge :].T, forward))
        mixed.append(mix(span, q, rim, filtered[h], coefficients[lanes]))

    results = []
    for c in range(chunks):
        sums = output_sums(order, mixed, outs[c])
        if c + 1 < chunks or chunks == 1:
            total = sum_over_y(places, sums, y)
            part = total.shape[0] // 2
            result = sum_over_zl(
                places, take(total, core, part), take(total, 1 - core, part), home
            )
        else:
            quarters = sums.reshape(ny, 2, rows // (2 * ny), -1)
            pick = lambda index: lax.dynamic_index_in_dim(quarters, index, 1, keepdims=False)
            total = sum_over_zl(places, pick(core), pick(1 - core), home)
            total = total.reshape(rows // 2, -1).astype(BF16)
            result = sum_over_y(places, total, y)
        results.append(result.astype(BF16).reshape(result.shape[0], places.ctx, 1, chunk))
    return jnp.concatenate(results, axis=2).reshape(rows // places.tp, -1)


def solution(mesh):
    in_specs = (
        P("ctx", None),
        P(None, "ctx", "tp"),
        P(None, None, "tp"),
        P("tp", None),
        P("tp"),
        P("tp"),
        P("tp", "ctx"),
    )
    places = Places(mesh.shape["ctx"], mesh.shape["tp"])
    return jax.shard_map(
        functools.partial(per_device, places),
        mesh=mesh,
        in_specs=in_specs,
        out_specs=P(AXES, None),
        check_vma=False,
    )
```

time: 743 us -> 504 us (0.68)
  waiting for transfers between devices: 649 us -> 246 us
  Pallas kernels: 0 us -> 102 us
  starting transfers between devices: 4.03 us -> 71.6 us
  matrix products: 48.1 us -> 2.07 us
  other arithmetic: 12.7 us -> 35.8 us
  local copies, waits for them, and re-layouts: 14.2 us -> 36.2 us
  between operations: 13.3 us -> 1.44 us
    all_gather x2 -> x0, waiting for transfers between devices: 536 us -> none  [the longest x1 481 us: per_device(): lax.all_gather(qkv_weight, 'ctx', axis=1, tiled=True)]
    ppermute x2 -> x53, waiting for transfers between devices: 12 us -> 246 us  [the longest x18 144 us: deliver(): return lax.ppermute(value, AXES, pairs)]
    pallas_call x0 -> x13, Pallas kernels: none -> 102 us  [the longest x6 47.2 us: project(): pl.pallas_call(project_kernel, out_shape=jax.ShapeDtypeStruct((width, row...]
    reduce_scatter x1 -> x0, waiting for transfers between devices: 98.7 us -> none  [per_device(): lax.psum_scatter(lax.dot_general(mixed, out_rows, (((0,), (0,)), ((), ())...]
    ppermute x2 -> x53, starting transfers between devices: 3.95 us -> 71.6 us  [the longest x18 37.6 us: deliver(): return lax.ppermute(value, AXES, pairs)]
    dot_general x5 -> x1, matrix products: 48.1 us -> 2.07 us  [bands_of(): jnp.einsum('gk,kji->gji', filters, picker, preferred_element_type=F32)]
    another operation x0 -> x18, other arithmetic: none -> 11.2 us  [the longest x16 7.43 us: gather(): held = jnp.stack([jnp.where(home, shard, near)] + far)]
    unnamed x19 -> x62, local copies, waits for them, and re-layouts: 1.53 us -> 9.37 us
  transfers between devices with their start and end apart: 5 -> 53, of which waited for: 5 -> 19; matrix products, arithmetic and copies ran while one was open for 8% -> 12% of each run, Pallas kernels for 0% -> 21%
where the time goes in v1:
time: 504 us; the launch traced here: 495 us
  waiting for transfers between devices  246 us (49%)
  Pallas kernels  102 us (20%)
  starting transfers between devices  71.6 us (14%)
  local copies, waits for them, and re-layouts  36.2 us (7%)
  other arithmetic  35.8 us (7%)
    ppermute x18, waiting for transfers between devices, deliver(): return lax.ppermute(value, AXES, pairs)  144 us
    ppermute x35, waiting for transfers between devices, send(): return lax.ppermute(value, AXES, pairs)  102 us
    pallas_call x6, Pallas kernels, project(): pl.pallas_call(project_kernel, out_shape=jax.ShapeDtypeStruct((width, row...  47.2 us
    ppermute x18, starting transfers between devices, deliver(): return lax.ppermute(value, AXES, pairs)  37.6 us
    ppermute x35, starting transfers between devices, send(): return lax.ppermute(value, AXES, pairs)  34 us
    pallas_call x2, Pallas kernels, output_sums(): pl.pallas_call(functools.partial(output_kernel, len(mixed)), out_shape=ja...  16.1 us
    pallas_call x2, Pallas kernels, long_filter_part(): pl.pallas_call(functools.partial(filter_kernel, span), out_shape=jax.Shap...  16 us
    pallas_call x1, Pallas kernels, prepare(): pl.pallas_call(functools.partial(prepare_kernel, per_part), out_shape=jax...  11.4 us
  transfers between devices with their start and end apart: 53, of which 19 were waited for; matrix products, arithmetic and copies ran while one was open for 12% of the time, Pallas kernels for 21%

profile of v1, /device:TPU:17, one launch (start us, length us, event | category | flops | bytes accessed | tf_op | source)
XLA Modules:
  0.0 494.8 jit_solution(9453907057221125219)
XLA Ops:
  25.2 74.1 %collective-permute-done.20 = f32[30,1024]{0,1:T(8,128)} collective-permute-done((f32[30,1024]{0,1:T(8,128)}, f32[30,1024]{0,1:T(8,128)}, u32[]{:S(2)}, u32[]{:S(2)}) %collective-permute-start.20) | collective-permute-done | bytes 122912 | tf_op jit(solution)/shard_map/ppermute | solution.py:41
  118.2 19.8 %collective-permute-done.6 = bf16[512,512]{1,0:T(8,128)(2,1)S(1)} collective-permute-done((bf16[512,512]{1,0:T(8,128)(2,1)}, bf16[512,512]{1,0:T(8,128)(2,1)S(1)}, u32[]{:S(2)}, u32[]{:S(2)}) %collective-permute-start.6) | collective-permute-done | bytes 524320 | tf_op jit(solution)/shard_map/ppermute | solution.py:41
  139.9 8.4 %collective-permute-done.3 = bf16[512,512]{1,0:T(8,128)(2,1)S(1)} collective-permute-done((bf16[512,512]{1,0:T(8,128)(2,1)}, bf16[512,512]{1,0:T(8,128)(2,1)S(1)}, u32[]{:S(2)}, u32[]{:S(2)}) %collective-permute-start.3) | collective-permute-done | bytes 524320 | tf_op jit(solution)/shard_map/ppermute | solution.py:41
  153.6 23.8 %collective-permute-done.23 = bf16[512,512]{1,0:T(8,128)(2,1)S(1)} collective-permute-done((bf16[512,512]{1,0:T(8,128)(2,1)S(1)}, bf16[512,512]{1,0:T(8,128)(2,1)S(1)}, u32[]{:S(2)}, u32[]{:S(2)}) %collective-permute-start.23) | collective-permute-done | bytes 524320 | tf_op jit(solution)/shard_map/ppermute | solution.py:41
  210.5 7.2 %collective-permute-done.46 = bf16[1024,256]{1,0:T(8,128)(2,1)S(1)} collective-permute-done((bf16[1024,256]{1,0:T(8,128)(2,1)S(1)}, bf16[1024,256]{1,0:T(8,128)(2,1)S(1)}, u32[]{:S(2)}, u32[]{:S(2)}) %collective-permute-start.46) | collective-permute-done | bytes 524320 | tf_op jit(solution)/shard_map/ppermute | solution.py:41
  221.0 11.4 %shard_map.73.tokens = bf16[4096,768]{1,0:T(8,128)(2,1)} custom-call(s32[8]{0:T(128)} %stack.119.order, s32[2]{0:T(128)} %pad_add_fusion.flags, bf16[768,4096]{1,0:T(8,128)(2,1)} %own.1, bf16[768,2048]{1,0:T(8,128)(2,1)} %collective-permute-done.refs_0_, bf16[768,2048]{1,0:T(8,128)(2,1)} %copy-done.6), custom_call_target="tpu_custom_call" | custom-call | bytes 18874368 | tf_op jit(solution)/shard_map/pallas_call | solution.py:94
  232.5 7.9 %shard_map.81.v = bf16[512,768]{1,0:T(8,128)(2,1)} custom-call(bf16[4096,768]{1,0:T(8,128)(2,1)} %shard_map.73.tokens, bf16[2,512,512]{2,1,0:T(8,128)(2,1)} %pad_maximum_fusion.7.refs_0_, bf16[2,512,512]{2,1,0:T(8,128)(2,1)} %collective-permute-done.33.refs_1_, bf16[2,512,512]{2,1,0:T(8,128)(2,1)} %collective-permute-done.34.refs_2_, ...), custom_call_target="tpu_custom_call" | custom-call | flops 3221225472 | bytes 11272192 | tf_op jit(solution)/shard_map/pallas_call | solution.py:123
  242.6 7.8 %shard_map.80.k = bf16[512,768]{1,0:T(8,128)(2,1)} custom-call(bf16[4096,768]{1,0:T(8,128)(2,1)} %shard_map.73.tokens, bf16[2,512,512]{2,1,0:T(8,128)(2,1)} %copy-done.17, bf16[2,512,512]{2,1,0:T(8,128)(2,1)} %collective-permute-done.29.refs_1_, bf16[2,512,512]{2,1,0:T(8,128)(2,1)} %collective-permute-done.30.refs_2_, ...), custom_call_target="tpu_custom_call" | custom-call | flops 3221225472 | bytes 11272192 | tf_op jit(solution)/shard_map/pallas_call | solution.py:123
  251.8 10.0 %collective-permute-done.13.refs_1_ = bf16[2,512,512]{2,1,0:T(8,128)(2,1)} collective-permute-done((bf16[2,512,512]{2,1,0:T(8,128)(2,1)S(1)}, bf16[2,512,512]{2,1,0:T(8,128)(2,1)}, u32[]{:S(2)}, u32[]{:S(2)}) %collective-permute-start.13) | collective-permute-done | bytes 1048608 | tf_op jit(solution)/shard_map/ppermute | solution.py:50
  267.7 7.8 %shard_map.76.v = bf16[512,768]{1,0:T(8,128)(2,1)} custom-call(bf16[4096,768]{1,0:T(8,128)(2,1)} %shard_map.73.tokens, bf16[2,512,512]{2,1,0:T(8,128)(2,1)} %pad_maximum_fusion.4.refs_0_, bf16[2,512,512]{2,1,0:T(8,128)(2,1)} %collective-permute-done.17.refs_1_, bf16[2,512,512]{2,1,0:T(8,128)(2,1)} %collective-permute-done.18.refs_2_, ...), custom_call_target="tpu_custom_call" | custom-call | flops 3221225472 | bytes 11272192 | tf_op jit(solution)/shard_map/pallas_call | solution.py:123
  275.6 8.7 %collective-permute-done.24.refs_1_ = bf16[2,512,512]{2,1,0:T(8,128)(2,1)} collective-permute-done((bf16[2,512,512]{2,1,0:T(8,128)(2,1)S(1)}, bf16[2,512,512]{2,1,0:T(8,128)(2,1)}, u32[]{:S(2)}, u32[]{:S(2)}) %collective-permute-start.24) | collective-permute-done | bytes 1048608 | tf_op jit(solution)/shard_map/ppermute | solution.py:50
  287.0 19.8 %collective-permute-done.8.refs_1_ = bf16[2,512,512]{2,1,0:T(8,128)(2,1)} collective-permute-done((bf16[2,512,512]{2,1,0:T(8,128)(2,1)S(1)}, bf16[2,512,512]{2,1,0:T(8,128)(2,1)}, u32[]{:S(2)}, u32[]{:S(2)}) %collective-permute-start.8) | collective-permute-done | bytes 1048608 | tf_op jit(solution)/shard_map/ppermute | solution.py:50
  306.8 7.8 %shard_map.75.k = bf16[512,768]{1,0:T(8,128)(2,1)} custom-call(bf16[4096,768]{1,0:T(8,128)(2,1)} %shard_map.73.tokens, bf16[2,512,512]{2,1,0:T(8,128)(2,1)} %copy-done.16, bf16[2,512,512]{2,1,0:T(8,128)(2,1)} %collective-permute-done.13.refs_1_, bf16[2,512,512]{2,1,0:T(8,128)(2,1)} %copy-done.25, bf16[2,512,512]{2,1,0:T(8,128)(2,1)} %collective-permute-done.15.refs_3_), custom_call_target="tpu_custom_call" | custom-call | flops 3221225472 | bytes 11272192 | tf_op jit(solution)/shard_map/pallas_call | solution.py:123
  317.3 9.1 %collective-permute-done.39.refs_3_ = bf16[2,1024,256]{2,1,0:T(8,128)(2,1)S(1)} collective-permute-done((bf16[2,1024,256]{2,1,0:T(8,128)(2,1)S(1)}, bf16[2,1024,256]{2,1,0:T(8,128)(2,1)S(1)}, u32[]{:S(2)}, u32[]{:S(2)}) %collective-permute-start.39) | collective-permute-done | bytes 1048608 | tf_op jit(solution)/shard_map/ppermute | solution.py:50
  327.8 7.8 %shard_map.79.q = bf16[512,768]{1,0:T(8,128)(2,1)} custom-call(bf16[4096,768]{1,0:T(8,128)(2,1)} %shard_map.73.tokens, bf16[2,512,512]{2,1,0:T(8,128)(2,1)} %copy-done.18, bf16[2,512,512]{2,1,0:T(8,128)(2,1)} %collective-permute-done.24.refs_1_, bf16[2,512,512]{2,1,0:T(8,128)(2,1)} %collective-permute-done.25.refs_2_, ...), custom_call_target="tpu_custom_call" | custom-call | flops 3221225472 | bytes 11272192 | tf_op jit(solution)/shard_map/pallas_call | solution.py:123
  342.9 8.1 %shard_map.74.q = bf16[512,768]{1,0:T(8,128)(2,1)} custom-call(bf16[4096,768]{1,0:T(8,128)(2,1)} %shard_map.73.tokens, bf16[2,512,512]{2,1,0:T(8,128)(2,1)} %copy-done.15, bf16[2,512,512]{2,1,0:T(8,128)(2,1)} %collective-permute-done.8.refs_1_, bf16[2,512,512]{2,1,0:T(8,128)(2,1)} %collective-permute-done.9.refs_2_, ...), custom_call_target="tpu_custom_call" | custom-call | flops 3221225472 | bytes 11272192 | tf_op jit(solution)/shard_map/pallas_call | solution.py:123
  352.0 6.8 %collective-permute-done.27 = bf16[8,512]{0,1:T(8,128)(2,1)S(1)} collective-permute-done((bf16[8,512]{0,1:T(8,128)(2,1)S(1)}, bf16[8,512]{0,1:T(8,128)(2,1)S(1)}, u32[]{:S(2)}, u32[]{:S(2)}) %collective-permute-start.27) | collective-permute-done | bytes 8224 | tf_op jit(solution)/shard_map/ppermute | solution.py:50
  377.6 8.0 %shard_map.82.filtered = f32[512,768]{1,0:T(8,128)} custom-call(bf16[512,768]{1,0:T(8,128)(2,1)} %shard_map.80.k, bf16[512,768]{1,0:T(8,128)(2,1)} %shard_map.81.v, bf16[512,128]{1,0:T(8,128)(2,1)} %pad.28.k_rim, bf16[512,128]{1,0:T(8,128)(2,1)} %pad.29.v_rim, bf16[512,128]{1,0:T(8,128)(2,1)} %slice_bitcast_fusion.1.before, ...), custom_call_target="tpu_custom_call" | custom-call | flops 223346688 | bytes 5242880 | tf_op jit(solution)/shard_map/pallas_call | solution.py:177
  393.2 8.0 %shard_map.77.filtered = f32[512,768]{1,0:T(8,128)} custom-call(bf16[512,768]{1,0:T(8,128)(2,1)} %shard_map.75.k, bf16[512,768]{1,0:T(8,128)(2,1)} %shard_map.76.v, bf16[512,128]{1,0:T(8,128)(2,1)} %pad.24.k_rim, bf16[512,128]{1,0:T(8,128)(2,1)} %pad.25.v_rim, bf16[512,128]{1,0:T(8,128)(2,1)} %slice_bitcast_fusion.7.before, ...), custom_call_target="tpu_custom_call" | custom-call | flops 223346688 | bytes 5242880 | tf_op jit(solution)/shard_map/pallas_call | solution.py:177
  407.6 8.0 %shard_map.84 = bf16[768,2048]{1,0:T(8,128)(2,1)} custom-call(s32[8]{0:T(128)} %stack.119.order, bf16[768,512]{1,0:T(8,128)(2,1)} %shard_map.78.refs_0_, bf16[768,512]{1,0:T(8,128)(2,1)} %shard_map.83.refs_1_, bf16[2,1024,256]{2,1,0:T(8,128)(2,1)} %copy-done.14, bf16[2,1024,256]{2,1,0:T(8,128)(2,1)} %copy-done.23, bf16[2,1024,256]{2,1,0:T(8,128)(2,1)} %copy-done.24, ...), custom_call_target="tpu_custom_call" | custom-call | flops 3221225472 | bytes 8912896 | tf_op jit(solution)/shard_map/pallas_call | solution.py:237
  418.5 8.1 %shard_map.85 = bf16[768,2048]{1,0:T(8,128)(2,1)} custom-call(s32[8]{0:T(128)} %stack.119.order, bf16[768,512]{1,0:T(8,128)(2,1)} %shard_map.78.refs_0_, bf16[768,512]{1,0:T(8,128)(2,1)} %shard_map.83.refs_1_, bf16[2,1024,256]{2,1,0:T(8,128)(2,1)} %copy-done.13, bf16[2,1024,256]{2,1,0:T(8,128)(2,1)} %collective-permute-done.47.refs_3_, ...), custom_call_target="tpu_custom_call" | custom-call | flops 3221225472 | bytes 8912896 | tf_op jit(solution)/shard_map/pallas_call | solution.py:237
  435.7 18.0 %collective-permute-done.42 = bf16[384,2048]{1,0:T(8,128)(2,1)} collective-permute-done((bf16[384,2048]{1,0:T(8,128)(2,1)S(1)}, bf16[384,2048]{1,0:T(8,128)(2,1)}, u32[]{:S(2)}, u32[]{:S(2)}) %collective-permute-start.42) | collective-permute-done | bytes 1572896 | tf_op jit(solution)/shard_map/ppermute | solution.py:50
  462.0 7.3 %collective-permute-done.51 = bf16[2,192,2048]{2,1,0:T(8,128)(2,1)} collective-permute-done((bf16[2,192,2048]{2,1,0:T(8,128)(2,1)}, bf16[2,192,2048]{2,1,0:T(8,128)(2,1)}, u32[]{:S(2)}, u32[]{:S(2)}) %collective-permute-start.51) | collective-permute-done | bytes 1572896 | tf_op jit(solution)/shard_map/ppermute | solution.py:50
  474.1 11.7 %collective-permute-done.44 = bf16[192,2048]{1,0:T(8,128)(2,1)} collective-permute-done((bf16[192,2048]{1,0:T(8,128)(2,1)}, bf16[192,2048]{1,0:T(8,128)(2,1)}, u32[]{:S(2)}, u32[]{:S(2)}) %collective-permute-start.44) | collective-permute-done | bytes 786464 | tf_op jit(solution)/shard_map/ppermute | solution.py:50
  (234 shorter events, 177.9 us)
Async XLA Ops:
  4.1 102.0 %collective-permute-start = (bf16[768,2048]{1,0:T(8,128)(2,1)}, bf16[768,2048]{1,0:T(8,128)(2,1)}, u32[]{:S(2)}, u32[]{:S(2)}) collective-permute-start(bf16[768,2048]{1,0:T(8,128)(2,1)} %constant_dynamic-slice_fusion.2), channel_id=1, source_target_pairs={{1,8},{3,10},{5,12},{7,14},{8,1},{10,3},{12,5},{14,7},{17,24},{19,... | collective-permute-start | bytes 9437192 | tf_op jit(solution)/shard_map/ppermute | solution.py:41
  9.2 100.2 %collective-permute-start.5 = (bf16[512,512]{1,0:T(8,128)(2,1)}, bf16[512,512]{1,0:T(8,128)(2,1)}, u32[]{:S(2)}, u32[]{:S(2)}) collective-permute-start(bf16[512,512]{1,0:T(8,128)(2,1)} %bitcast.148), channel_id=1, source_target_pairs={{0,16},{1,24},{2,18},{3,26},{4,20},{5,28},{6,22},{7,30},{8,17},{9,... | collective-permute-start | bytes 1572872 | tf_op jit(solution)/shard_map/ppermute | solution.py:41
  9.2 140.9 %collective-permute-start.12 = (bf16[512,512]{1,0:T(8,128)(2,1)}, bf16[512,512]{1,0:T(8,128)(2,1)}, u32[]{:S(2)}, u32[]{:S(2)}) collective-permute-start(bf16[512,512]{1,0:T(8,128)(2,1)} %bitcast.149), channel_id=1, source_target_pairs={{1,8},{3,10},{5,12},{7,14},{8,1},{10,3},{12,5},{14,7},{17,24},{19,... | collective-permute-start | bytes 1572872 | tf_op jit(solution)/shard_map/ppermute | solution.py:41
  13.7 96.7 %collective-permute-start.2 = (bf16[512,512]{1,0:T(8,128)(2,1)}, bf16[512,512]{1,0:T(8,128)(2,1)}, u32[]{:S(2)}, u32[]{:S(2)}) collective-permute-start(bf16[512,512]{1,0:T(8,128)(2,1)} %bitcast.16), channel_id=1, source_target_pairs={{0,16},{1,24},{2,18},{3,26},{4,20},{5,28},{6,22},{7,30},{8,17},{9,... | collective-permute-start | bytes 1572872 | tf_op jit(solution)/shard_map/ppermute | solution.py:41
  16.1 83.3 %collective-permute-start.20 = (f32[30,1024]{0,1:T(8,128)}, f32[30,1024]{0,1:T(8,128)}, u32[]{:S(2)}, u32[]{:S(2)}) collective-permute-start(f32[30,1024]{0,1:T(8,128)} %copy.38), channel_id=1, source_target_pairs={{1,8},{3,10},{5,12},{7,14},{8,1},{10,3},{12,5},{14,7},{17,24},{19,... | collective-permute-start | bytes 368648 | tf_op jit(solution)/shard_map/ppermute | solution.py:41
  106.1 112.9 %collective-permute-start.1 = (bf16[768,2048]{1,0:T(8,128)(2,1)}, bf16[768,2048]{1,0:T(8,128)(2,1)S(1)}, u32[]{:S(2)}, u32[]{:S(2)}) collective-permute-start(bf16[768,2048]{1,0:T(8,128)(2,1)} %collective-permute-done.refs_0_), channel_id=1, source_target_pairs={{8,10},{10,8},{12,14},{14,12},{1,3},{3,1},{5,7},{7,5},{24,26},{26,... | collective-permute-start | bytes 9437192 | tf_op jit(solution)/shard_map/ppermute | solution.py:50
  110.5 37.9 %collective-permute-start.3 = (bf16[512,512]{1,0:T(8,128)(2,1)}, bf16[512,512]{1,0:T(8,128)(2,1)S(1)}, u32[]{:S(2)}, u32[]{:S(2)}) collective-permute-start(bf16[512,512]{1,0:T(8,128)(2,1)} %bitcast.152), channel_id=1, source_target_pairs={{0,16},{1,24},{2,18},{3,26},{4,20},{5,28},{6,22},{7,30},{8,17},{9,... | collective-permute-start | bytes 1572872 | tf_op jit(solution)/shard_map/ppermute | solution.py:41
  111.3 40.0 %collective-permute-start.28 = (bf16[512,512]{1,0:T(8,128)(2,1)}, bf16[512,512]{1,0:T(8,128)(2,1)S(1)}, u32[]{:S(2)}, u32[]{:S(2)}) collective-permute-start(bf16[512,512]{1,0:T(8,128)(2,1)} %bitcast.155), channel_id=1, source_target_pairs={{1,8},{3,10},{5,12},{7,14},{8,1},{10,3},{12,5},{14,7},{17,24},{19,... | collective-permute-start | bytes 1572872 | tf_op jit(solution)/shard_map/ppermute | solution.py:41
  138.0 41.4 %collective-permute-start.32 = (bf16[512,512]{1,0:T(8,128)(2,1)S(1)}, bf16[512,512]{1,0:T(8,128)(2,1)S(1)}, u32[]{:S(2)}, u32[]{:S(2)}) collective-permute-start(bf16[512,512]{1,0:T(8,128)(2,1)S(1)} %bitcast.153), channel_id=1, source_target_pairs={{1,8},{3,10},{5,12},{7,14},{8,1},{10,3},{12,5},{14,7},{17,24},{19,... | collective-permute-start | bytes 1572872 | tf_op jit(solution)/shard_map/ppermute | solution.py:41
  240.4 35.1 %collective-permute-start.14 = (bf16[2,512,512]{2,1,0:T(8,128)(2,1)S(1)}, bf16[2,512,512]{2,1,0:T(8,128)(2,1)S(1)}, u32[]{:S(2)}, u32[]{:S(2)}) collective-permute-start(bf16[2,512,512]{2,1,0:T(8,128)(2,1)S(1)} %pad_maximum_fusion.3.refs_0_), channel_id=1, source_target_pairs={{0,1},{8,9},{2,3},{10,11},{4,5},{12,13},{6,7},{14,15},{1,0},{9,8},... | collective-permute-start | bytes 3145736 | tf_op jit(solution)/shard_map/ppermute | solution.py:50
  240.9 43.4 %collective-permute-start.24 = (bf16[2,512,512]{2,1,0:T(8,128)(2,1)S(1)}, bf16[2,512,512]{2,1,0:T(8,128)(2,1)}, u32[]{:S(2)}, u32[]{:S(2)}) collective-permute-start(bf16[2,512,512]{2,1,0:T(8,128)(2,1)S(1)} %pad_maximum_fusion.5.refs_0_), channel_id=1, source_target_pairs={{0,4},{8,12},{2,6},{10,14},{4,0},{12,8},{6,2},{14,10},{1,5},{9,13}... | collective-permute-start | bytes 3145736 | tf_op jit(solution)/shard_map/ppermute | solution.py:50
  261.8 44.9 %collective-permute-start.8 = (bf16[2,512,512]{2,1,0:T(8,128)(2,1)S(1)}, bf16[2,512,512]{2,1,0:T(8,128)(2,1)}, u32[]{:S(2)}, u32[]{:S(2)}) collective-permute-start(bf16[2,512,512]{2,1,0:T(8,128)(2,1)S(1)} %pad_maximum_fusion.2.refs_0_), channel_id=1, source_target_pairs={{0,4},{8,12},{2,6},{10,14},{4,0},{12,8},{6,2},{14,10},{1,5},{9,13}... | collective-permute-start | bytes 3145736 | tf_op jit(solution)/shard_map/ppermute | solution.py:50
  267.1 49.6 %collective-permute-start.25 = (bf16[2,512,512]{2,1,0:T(8,128)(2,1)S(1)}, bf16[2,512,512]{2,1,0:T(8,128)(2,1)}, u32[]{:S(2)}, u32[]{:S(2)}) collective-permute-start(bf16[2,512,512]{2,1,0:T(8,128)(2,1)S(1)} %pad_maximum_fusion.5.refs_0_), channel_id=1, source_target_pairs={{0,1},{8,9},{2,3},{10,11},{4,5},{12,13},{6,7},{14,15},{1,0},{9,8},... | collective-permute-start | bytes 3145736 | tf_op jit(solution)/shard_map/ppermute | solution.py:50
  275.5 50.9 %collective-permute-start.39 = (bf16[2,1024,256]{2,1,0:T(8,128)(2,1)S(1)}, bf16[2,1024,256]{2,1,0:T(8,128)(2,1)S(1)}, u32[]{:S(2)}, u32[]{:S(2)}) collective-permute-start(bf16[2,1024,256]{2,1,0:T(8,128)(2,1)S(1)} %pad_maximum_fusion.8.refs_2_), channel_id=1, source_target_pairs={{0,4},{8,12},{2,6},{10,14},{4,0},{12,8},{6,2},{14,10},{1,5},{9,13}... | collective-permute-start | bytes 3145736 | tf_op jit(solution)/shard_map/ppermute | solution.py:50
  284.3 43.5 %collective-permute-start.26 = (bf16[2,512,512]{2,1,0:T(8,128)(2,1)}, bf16[2,512,512]{2,1,0:T(8,128)(2,1)}, u32[]{:S(2)}, u32[]{:S(2)}) collective-permute-start(bf16[2,512,512]{2,1,0:T(8,128)(2,1)} %collective-permute-done.24.refs_1_), channel_id=1, source_target_pairs={{0,1},{8,9},{2,3},{10,11},{4,5},{12,13},{6,7},{14,15},{1,0},{9,8},... | collective-permute-start | bytes 3145736 | tf_op jit(solution)/shard_map/ppermute | solution.py:50
  286.4 52.3 %collective-permute-start.9 = (bf16[2,512,512]{2,1,0:T(8,128)(2,1)S(1)}, bf16[2,512,512]{2,1,0:T(8,128)(2,1)}, u32[]{:S(2)}, u32[]{:S(2)}) collective-permute-start(bf16[2,512,512]{2,1,0:T(8,128)(2,1)S(1)} %pad_maximum_fusion.2.refs_0_), channel_id=1, source_target_pairs={{0,1},{8,9},{2,3},{10,11},{4,5},{12,13},{6,7},{14,15},{1,0},{9,8},... | collective-permute-start | bytes 3145736 | tf_op jit(solution)/shard_map/ppermute | solution.py:50
  306.8 34.2 %collective-permute-start.10 = (bf16[2,512,512]{2,1,0:T(8,128)(2,1)}, bf16[2,512,512]{2,1,0:T(8,128)(2,1)}, u32[]{:S(2)}, u32[]{:S(2)}) collective-permute-start(bf16[2,512,512]{2,1,0:T(8,128)(2,1)} %collective-permute-done.8.refs_1_), channel_id=1, source_target_pairs={{0,1},{8,9},{2,3},{10,11},{4,5},{12,13},{6,7},{14,15},{1,0},{9,8},... | collective-permute-start | bytes 3145736 | tf_op jit(solution)/shard_map/ppermute | solution.py:50
  316.7 90.0 %collective-permute-start.40 = (bf16[2,1024,256]{2,1,0:T(8,128)(2,1)S(1)}, bf16[2,1024,256]{2,1,0:T(8,128)(2,1)S(1)}, u32[]{:S(2)}, u32[]{:S(2)}) collective-permute-start(bf16[2,1024,256]{2,1,0:T(8,128)(2,1)S(1)} %pad_maximum_fusion.8.refs_2_), channel_id=1, source_target_pairs={{0,1},{8,9},{2,3},{10,11},{4,5},{12,13},{6,7},{14,15},{1,0},{9,8},... | collective-permute-start | bytes 3145736 | tf_op jit(solution)/shard_map/ppermute | solution.py:50
  326.4 35.2 %collective-permute-start.47 = (bf16[2,1024,256]{2,1,0:T(8,128)(2,1)S(1)}, bf16[2,1024,256]{2,1,0:T(8,128)(2,1)}, u32[]{:S(2)}, u32[]{:S(2)}) collective-permute-start(bf16[2,1024,256]{2,1,0:T(8,128)(2,1)S(1)} %pad_maximum_fusion.9.refs_2_), channel_id=1, source_target_pairs={{0,4},{8,12},{2,6},{10,14},{4,0},{12,8},{6,2},{14,10},{1,5},{9,13}... | collective-permute-start | bytes 3145736 | tf_op jit(solution)/shard_map/ppermute | solution.py:50
  327.8 78.9 %collective-permute-start.41 = (bf16[2,1024,256]{2,1,0:T(8,128)(2,1)S(1)}, bf16[2,1024,256]{2,1,0:T(8,128)(2,1)}, u32[]{:S(2)}, u32[]{:S(2)}) collective-permute-start(bf16[2,1024,256]{2,1,0:T(8,128)(2,1)S(1)} %collective-permute-done.39.refs_3_), channel_id=1, source_target_pairs={{0,1},{8,9},{2,3},{10,11},{4,5},{12,13},{6,7},{14,15},{1,0},{9,8},... | collective-permute-start | bytes 3145736 | tf_op jit(solution)/shard_map/ppermute | solution.py:50
  361.6 56.9 %collective-permute-start.48 = (bf16[2,1024,256]{2,1,0:T(8,128)(2,1)S(1)}, bf16[2,1024,256]{2,1,0:T(8,128)(2,1)}, u32[]{:S(2)}, u32[]{:S(2)}) collective-permute-start(bf16[2,1024,256]{2,1,0:T(8,128)(2,1)S(1)} %pad_maximum_fusion.9.refs_2_), channel_id=1, source_target_pairs={{0,1},{8,9},{2,3},{10,11},{4,5},{12,13},{6,7},{14,15},{1,0},{9,8},... | collective-permute-start | bytes 3145736 | tf_op jit(solution)/shard_map/ppermute | solution.py:50
  366.2 52.3 %collective-permute-start.49 = (bf16[2,1024,256]{2,1,0:T(8,128)(2,1)}, bf16[2,1024,256]{2,1,0:T(8,128)(2,1)}, u32[]{:S(2)}, u32[]{:S(2)}) collective-permute-start(bf16[2,1024,256]{2,1,0:T(8,128)(2,1)} %collective-permute-done.47.refs_3_), channel_id=1, source_target_pairs={{0,1},{8,9},{2,3},{10,11},{4,5},{12,13},{6,7},{14,15},{1,0},{9,8},... | collective-permute-start | bytes 3145736 | tf_op jit(solution)/shard_map/ppermute | solution.py:50
  417.2 36.5 %collective-permute-start.42 = (bf16[384,2048]{1,0:T(8,128)(2,1)S(1)}, bf16[384,2048]{1,0:T(8,128)(2,1)}, u32[]{:S(2)}, u32[]{:S(2)}) collective-permute-start(bf16[384,2048]{1,0:T(8,128)(2,1)S(1)} %constant_dynamic-slice_fusion.1), channel_id=1, source_target_pairs={{0,2},{8,10},{2,0},{10,8},{4,6},{12,14},{6,4},{14,12},{1,3},{9,11}... | collective-permute-start | bytes 4718600 | tf_op jit(solution)/shard_map/ppermute | solution.py:50
  430.3 38.9 %collective-permute-start.51 = (bf16[2,192,2048]{2,1,0:T(8,128)(2,1)}, bf16[2,192,2048]{2,1,0:T(8,128)(2,1)}, u32[]{:S(2)}, u32[]{:S(2)}) collective-permute-start(bf16[2,192,2048]{2,1,0:T(8,128)(2,1)} %get-tuple-element.32), channel_id=1, source_target_pairs={{8,1},{10,3},{12,5},{14,7},{1,8},{3,10},{5,12},{7,14},{24,17},{26,... | collective-permute-start | bytes 4718600 | tf_op jit(solution)/shard_map/ppermute | solution.py:50
  (56 other events, 1382.7 us)

commit v2 on v1

--- a/solution.py
+++ b/solution.py
@@ -10,7 +10,6 @@
 AXES = ("ctx", "tp")
 BF16, F32 = jnp.bfloat16, jnp.float32
 VMEM_LIMIT = 56 << 20
-IN_FLIGHT = 2
 
 
 class Places:
@@ -55,21 +54,52 @@
         return groups + [[m ^ self.nx for m in group] for group in groups]
 
 
-def after(value, done):
-    return lax.optimization_barrier((value, done))[0] if done is not None else value
-
-
-def gather(places, home, shard, line):
-    far = []
-    for step in range(1, places.ctx // (2 * places.nx)):
-        far.append(places.deliver(after(shard, line[-IN_FLIGHT]), step * 2 * places.nx))
-        line.append(far[-1])
-    near = places.deliver(after(shard, line[-IN_FLIGHT]))
-    held = jnp.stack([jnp.where(home, shard, near)] + far)
-    stacks = [held]
-    for step in range(1, places.nx):
-        stacks.append(places.send(held, lambda v, w, m=step: (v ^ m, w)))
-    return stacks + [places.send(stack, lambda v, w: (v ^ places.nx, w)) for stack in stacks]
+def after(value, *done):
+    done = [entry for group in done for entry in group]
+    return lax.optimization_barrier((value, *done))[0] if done else value
+
+
+class Line:
+    def __init__(self, places):
+        self.places, self.far, self.across, self.sibling = places, [], [], []
+
+    def so_far(self, history, lag):
+        return history[-lag] if len(history) >= lag else []
+
+    def gather(self, own, shard):
+        places = self.places
+        shard = after(
+            shard,
+            self.so_far(self.far, 2),
+            self.so_far(self.across, 2),
+            self.so_far(self.sibling, 3),
+        )
+        far = [
+            places.deliver(shard, step * 2 * places.nx)
+            for step in range(1, places.ctx // (2 * places.nx))
+        ]
+        self.far.append(far)
+        yield
+        held = jnp.stack([own] + far)
+        across = [
+            places.send(held, lambda v, w, m=step: (v ^ m, w)) for step in range(1, places.nx)
+        ]
+        self.across.append(across)
+        yield
+        both = jnp.concatenate([held] + across)
+        sibling = places.send(both, lambda v, w: (v ^ places.nx, w))
+        self.sibling.append([sibling])
+        yield [both, sibling]
+
+
+def run_line(jobs):
+    results = {}
+    for turn in range(len(jobs) + 2):
+        for lag in (2, 1, 0):
+            index = turn - lag
+            if 0 <= index < len(jobs):
+                results[index] = next(jobs[index])
+    return [results[index] for index in range(len(jobs))]
 
 
 def prepare_kernel(per_part, order, flags, own, *refs):
@@ -322,12 +352,13 @@
     order = jnp.stack([v ^ m for group in places.spread_masks() for m in group]).astype(jnp.int32)
     flags = jnp.stack([home.astype(jnp.int32), y.astype(jnp.int32)])
 
-    line = [None] * IN_FLIGHT
-    pieces = {}
-    pieces[1, 0] = gather(places, home, qkv_weight[1, :, :half].T, line)
+    line = Line(places)
+    first = qkv_weight[1].T
 
     share = in_features // ny
-    mine = places.deliver(lax.dynamic_slice_in_dim(tokens, y * share, share, 1))
+    mine = places.deliver(
+        lax.dynamic_slice_in_dim(after(tokens, [first]), y * share, share, 1)
+    )
     parts = [mine]
     for step in range(1, ny):
         parts.append(
@@ -338,12 +369,26 @@
         )
     tokens = prepare(order, flags, tokens, parts, depth)
 
-    for s, h in ((2, 0), (1, 1), (2, 1), (0, 0), (0, 1)):
-        pieces[s, h] = gather(places, home, qkv_weight[s, :, h * half : (h + 1) * half].T, line)
-    outs = [
-        gather(places, home, out_weight[:, c * chunk : (c + 1) * chunk], line)
-        for c in range(chunks)
-    ]
+    def weights(s, h, state):
+        if h == 0:
+            weight = qkv_weight[s] if s < 3 else out_weight
+            weight = after(weight, line.so_far(line.far, 1))
+            state[0] = weight.T if s < 3 else weight
+            state[1] = jnp.where(home, state[0], places.deliver(state[0]))
+        if s < 3:
+            own, shard = (entry[h * half : (h + 1) * half] for entry in (state[1], state[0]))
+        else:
+            own, shard = (entry[:, h * chunk : (h + 1) * chunk] for entry in (state[1], state[0]))
+        yield from line.gather(own, shard)
+
+    jobs, names = [], []
+    for s, count in ((1, 2), (2, 2), (0, 2), (3, chunks)):
+        state = [None, None]
+        for h in range(count):
+            jobs.append(weights(s, h, state))
+            names.append((s, h))
+    pieces = dict(zip(names, run_line(jobs)))
+    outs = [pieces[3, c] for c in range(chunks)]
 
     tap_index = jnp.arange(taps, dtype=F32)
     filters = (long_filter * jnp.exp(-decay_rate[:, None] * tap_index[None, :])).astype(BF16)
@@ -354,7 +399,11 @@
             filters.astype(F32).reshape(-1, width),
         ]
     )
-    packed = jnp.where(home, packed, places.deliver(packed))
+    packed = jnp.where(
+        home,
+        packed,
+        places.send(packed, lambda a, b: (a ^ nx, b) if places.at_home(a, b) else None),
+    )
     short = packed[: 3 * span].reshape(3, span, width)
     coefficients = jnp.pad(packed[: 3 * span + 1].T, ((0, 0), (0, (-3 * span - 1) % 8)))
     bands = bands_of(packed[3 * span + 1 :].reshape(groups, taps).astype(BF16))

time: 504 us -> 498 us (0.988)
  the two profiles are of different devices: /device:TPU:17 before, /device:TPU:0 now
where the time goes in v2:
time: 498 us; the launch traced here: 490 us
  waiting for transfers between devices  189 us (38%)
  starting transfers between devices  113 us (23%)
  Pallas kernels  101 us (20%)
  other arithmetic  48 us (10%)
  local copies, waits for them, and re-layouts  35.7 us (7%)
    ppermute x13, waiting for transfers between devices, deliver(): return lax.ppermute(value, AXES, pairs)  108 us
    ppermute x28, starting transfers between devices, send(): return lax.ppermute(value, AXES, pairs)  95.7 us
    ppermute x28, waiting for transfers between devices, send(): return lax.ppermute(value, AXES, pairs)  80.5 us
    pallas_call x6, Pallas kernels, project(): pl.pallas_call(project_kernel, out_shape=jax.ShapeDtypeStruct((width, row...  46.9 us
    ppermute x13, starting transfers between devices, deliver(): return lax.ppermute(value, AXES, pairs)  17.5 us
    pallas_call x2, Pallas kernels, output_sums(): pl.pallas_call(functools.partial(output_kernel, len(mixed)), out_shape=ja...  16.3 us
    pallas_call x2, Pallas kernels, long_filter_part(): pl.pallas_call(functools.partial(filter_kernel, span), out_shape=jax.Shap...  16 us
    concatenate x8, other arithmetic, gather(): both = jnp.concatenate([held] + across)  13.7 us
  transfers between devices with their start and end apart: 41, of which 15 were waited for; matrix products, arithmetic and copies ran while one was open for 15% of the time, Pallas kernels for 21%

profile of v2, /device:TPU:0, one launch (start us, length us, event | category | flops | bytes accessed | tf_op | source)
XLA Modules:
  0.0 490.3 jit_solution(5047388228870216509)
XLA Ops:
  9.7 17.6 %collective-permute-done.2 = bf16[512,512]{1,0:T(8,128)(2,1)} collective-permute-done((bf16[512,512]{1,0:T(8,128)(2,1)}, bf16[512,512]{1,0:T(8,128)(2,1)}, u32[]{:S(2)}, u32[]{:S(2)}) %collective-permute-start.2) | collective-permute-done | bytes 524320 | tf_op jit(solution)/shard_map/ppermute | solution.py:40
  37.1 11.4 %collective-permute-start.18 = (f32[30,1024]{0,1:T(8,128)}, f32[30,1024]{0,1:T(8,128)}, u32[]{:S(2)}, u32[]{:S(2)}) collective-permute-start(f32[30,1024]{0,1:T(8,128)} %copy.30), channel_id=1, source_target_pairs={{0,1},{2,3},{4,5},{6,7},{9,8},{11,10},{13,12},{15,14},{16,17},{18,... | collective-permute-start | bytes 368648 | tf_op jit(solution)/shard_map/ppermute | solution.py:49
  59.7 31.0 %collective-permute-start.21 = (bf16[4,512,512]{2,1,0:T(8,128)(2,1)}, bf16[4,512,512]{2,1,0:T(8,128)(2,1)}, u32[]{:S(2)}, u32[]{:S(2)}) collective-permute-start(bf16[4,512,512]{2,1,0:T(8,128)(2,1)} %pad_maximum_fusion.4.refs_0_), channel_id=1, source_target_pairs={{0,1},{8,9},{2,3},{10,11},{4,5},{12,13},{6,7},{14,15},{1,0},{9,8},... | collective-permute-start | bytes 6291464 | tf_op jit(solution)/shard_map/ppermute | solution.py:49
  96.3 33.8 %collective-permute-done.5 = bf16[512,512]{1,0:T(8,128)(2,1)S(1)} collective-permute-done((bf16[512,512]{1,0:T(8,128)(2,1)S(1)}, bf16[512,512]{1,0:T(8,128)(2,1)S(1)}, u32[]{:S(2)}, u32[]{:S(2)}) %collective-permute-start.5) | collective-permute-done | bytes 524320 | tf_op jit(solution)/shard_map/ppermute | solution.py:40
  139.5 12.4 %collective-permute-done.20 = bf16[2,512,512]{2,1,0:T(8,128)(2,1)S(1)} collective-permute-done((bf16[2,512,512]{2,1,0:T(8,128)(2,1)S(1)}, bf16[2,512,512]{2,1,0:T(8,128)(2,1)S(1)}, u32[]{:S(2)}, u32[]{:S(2)}) %collective-permute-start.20) | collective-permute-done | bytes 1048608 | tf_op jit(solution)/shard_map/ppermute | solution.py:49
  154.3 11.3 %collective-permute-done.22 = bf16[512,512]{1,0:T(8,128)(2,1)S(1)} collective-permute-done((bf16[512,512]{1,0:T(8,128)(2,1)S(1)}, bf16[512,512]{1,0:T(8,128)(2,1)S(1)}, u32[]{:S(2)}, u32[]{:S(2)}) %collective-permute-start.22) | collective-permute-done | bytes 524320 | tf_op jit(solution)/shard_map/ppermute | solution.py:40
  176.5 23.0 %collective-permute-done.13 = bf16[512,512]{1,0:T(8,128)(2,1)S(1)} collective-permute-done((bf16[512,512]{1,0:T(8,128)(2,1)S(1)}, bf16[512,512]{1,0:T(8,128)(2,1)S(1)}, u32[]{:S(2)}, u32[]{:S(2)}) %collective-permute-start.13) | collective-permute-done | bytes 524320 | tf_op jit(solution)/shard_map/ppermute | solution.py:40
  201.9 11.3 %shard_map.73.tokens = bf16[4096,768]{1,0:T(8,128)(2,1)} custom-call(s32[8]{0:T(128)} %stack.119.order, s32[2]{0:T(128)} %pad_add_fusion.flags, bf16[768,4096]{1,0:T(8,128)(2,1)} %own.1, bf16[768,2048]{1,0:T(8,128)(2,1)} %collective-permute-done.refs_0_, bf16[768,2048]{1,0:T(8,128)(2,1)} %collective-permute-done.1.refs_1_), custom_call_target="tpu_custom_call" | custom-call | bytes 18874368 | tf_op jit(solution)/shard_map/pallas_call | solution.py:124
  213.1 7.8 %shard_map.76.v = bf16[512,768]{1,0:T(8,128)(2,1)} custom-call(bf16[4096,768]{1,0:T(8,128)(2,1)} %shard_map.73.tokens, bf16[4,512,512]{2,1,0:T(8,128)(2,1)} %pad_maximum_fusion.3.refs_0_, bf16[4,512,512]{2,1,0:T(8,128)(2,1)} %collective-permute-done.17.refs_1_), custom_call_target="tpu_custom_call" | custom-call | flops 3221225472 | bytes 11272192 | tf_op jit(solution)/shard_map/pallas_call | solution.py:153
  223.1 7.9 %shard_map.75.k = bf16[512,768]{1,0:T(8,128)(2,1)} custom-call(bf16[4096,768]{1,0:T(8,128)(2,1)} %shard_map.73.tokens, bf16[4,512,512]{2,1,0:T(8,128)(2,1)} %copy-done.5, bf16[4,512,512]{2,1,0:T(8,128)(2,1)} %copy-done.19), custom_call_target="tpu_custom_call" | custom-call | flops 3221225472 | bytes 11272192 | tf_op jit(solution)/shard_map/pallas_call | solution.py:153
  238.6 7.8 %shard_map.81.v = bf16[512,768]{1,0:T(8,128)(2,1)} custom-call(bf16[4096,768]{1,0:T(8,128)(2,1)} %shard_map.73.tokens, bf16[4,512,512]{2,1,0:T(8,128)(2,1)} %pad_maximum_fusion.6.refs_0_, bf16[4,512,512]{2,1,0:T(8,128)(2,1)} %collective-permute-done.26.refs_1_), custom_call_target="tpu_custom_call" | custom-call | flops 3221225472 | bytes 11272192 | tf_op jit(solution)/shard_map/pallas_call | solution.py:153
  249.6 7.8 %shard_map.80.k = bf16[512,768]{1,0:T(8,128)(2,1)} custom-call(bf16[4096,768]{1,0:T(8,128)(2,1)} %shard_map.73.tokens, bf16[4,512,512]{2,1,0:T(8,128)(2,1)} %pad_maximum_fusion.4.refs_0_, bf16[4,512,512]{2,1,0:T(8,128)(2,1)} %collective-permute-done.21.refs_1_), custom_call_target="tpu_custom_call" | custom-call | flops 3221225472 | bytes 11272192 | tf_op jit(solution)/shard_map/pallas_call | solution.py:153
  260.5 19.5 %collective-permute-done.35 = bf16[1024,256]{1,0:T(8,128)(2,1)S(1)} collective-permute-done((bf16[1024,256]{1,0:T(8,128)(2,1)}, bf16[1024,256]{1,0:T(8,128)(2,1)S(1)}, u32[]{:S(2)}, u32[]{:S(2)}) %collective-permute-start.35) | collective-permute-done | bytes 524320 | tf_op jit(solution)/shard_map/ppermute | solution.py:40
  314.1 12.1 %collective-permute-done.27 = bf16[144,512]{0,1:T(8,128)(2,1)S(1)} collective-permute-done((bf16[144,512]{0,1:T(8,128)(2,1)S(1)}, bf16[144,512]{0,1:T(8,128)(2,1)S(1)}, u32[]{:S(2)}, u32[]{:S(2)}) %collective-permute-start.27) | collective-permute-done | bytes 147488 | tf_op jit(solution)/shard_map/ppermute | solution.py:49
  328.5 8.0 %shard_map.77.filtered = f32[512,768]{1,0:T(8,128)} custom-call(bf16[512,768]{1,0:T(8,128)(2,1)} %shard_map.75.k, bf16[512,768]{1,0:T(8,128)(2,1)} %shard_map.76.v, bf16[512,128]{1,0:T(8,128)(2,1)} %pad.24.k_rim, bf16[512,128]{1,0:T(8,128)(2,1)} %pad.25.v_rim, bf16[512,128]{1,0:T(8,128)(2,1)} %slice_bitcast_fusion.15.before, ...), custom_call_target="tpu_custom_call" | custom-call | flops 223346688 | bytes 5242880 | tf_op jit(solution)/shard_map/pallas_call | solution.py:207
  340.1 7.8 %shard_map.74.q = bf16[512,768]{1,0:T(8,128)(2,1)} custom-call(bf16[4096,768]{1,0:T(8,128)(2,1)} %shard_map.73.tokens, bf16[4,512,512]{2,1,0:T(8,128)(2,1)} %copy-done.7, bf16[4,512,512]{2,1,0:T(8,128)(2,1)} %collective-permute-done.15.refs_1_), custom_call_target="tpu_custom_call" | custom-call | flops 3221225472 | bytes 11272192 | tf_op jit(solution)/shard_map/pallas_call | solution.py:153
  353.3 7.8 %shard_map.79.q = bf16[512,768]{1,0:T(8,128)(2,1)} custom-call(bf16[4096,768]{1,0:T(8,128)(2,1)} %shard_map.73.tokens, bf16[4,512,512]{2,1,0:T(8,128)(2,1)} %copy-done.6, bf16[4,512,512]{2,1,0:T(8,128)(2,1)} %collective-permute-done.24.refs_1_), custom_call_target="tpu_custom_call" | custom-call | flops 3221225472 | bytes 11272192 | tf_op jit(solution)/shard_map/pallas_call | solution.py:153
  364.0 8.0 %shard_map.82.filtered = f32[512,768]{1,0:T(8,128)} custom-call(bf16[512,768]{1,0:T(8,128)(2,1)} %shard_map.80.k, bf16[512,768]{1,0:T(8,128)(2,1)} %shard_map.81.v, bf16[512,128]{1,0:T(8,128)(2,1)} %pad.28.k_rim, bf16[512,128]{1,0:T(8,128)(2,1)} %pad.29.v_rim, bf16[512,128]{1,0:T(8,128)(2,1)} %slice_bitcast_fusion.9.before, ...), custom_call_target="tpu_custom_call" | custom-call | flops 223346688 | bytes 5242880 | tf_op jit(solution)/shard_map/pallas_call | solution.py:207
  384.5 8.2 %shard_map.85 = bf16[768,2048]{1,0:T(8,128)(2,1)} custom-call(s32[8]{0:T(128)} %stack.119.order, bf16[768,512]{1,0:T(8,128)(2,1)} %shard_map.78.refs_0_, bf16[768,512]{1,0:T(8,128)(2,1)} %shard_map.83.refs_1_, bf16[4,1024,256]{2,1,0:T(8,128)(2,1)} %pad_maximum_fusion.8.refs_2_, bf16[4,1024,256]{2,1,0:T(8,128)(2,1)} %collective-permute-done.37.refs_3_), custom_call_target="tpu_custom_call" | custom-call | flops 3221225472 | bytes 8912896 | tf_op jit(solution)/shard_map/pallas_call | solution.py:267
  398.2 10.4 %collective-permute-start.38 = (bf16[2,192,2048]{2,1,0:T(8,128)(2,1)}, bf16[2,192,2048]{2,1,0:T(8,128)(2,1)}, u32[]{:S(2)}, u32[]{:S(2)}) collective-permute-start(bf16[2,192,2048]{2,1,0:T(8,128)(2,1)} %get-tuple-element.25), channel_id=1, source_target_pairs={{0,1},{8,0},{2,3},{10,2},{4,5},{12,4},{6,7},{14,6},{1,9},{9,8},{3,... | collective-permute-start | bytes 4718600 | tf_op jit(solution)/shard_map/ppermute | solution.py:49
  408.6 8.1 %shard_map.84 = bf16[768,2048]{1,0:T(8,128)(2,1)} custom-call(s32[8]{0:T(128)} %stack.119.order, bf16[768,512]{1,0:T(8,128)(2,1)} %shard_map.78.refs_0_, bf16[768,512]{1,0:T(8,128)(2,1)} %shard_map.83.refs_1_, bf16[4,1024,256]{2,1,0:T(8,128)(2,1)} %pad_maximum_fusion.7.refs_2_, bf16[4,1024,256]{2,1,0:T(8,128)(2,1)} %collective-permute-done.31.refs_3_), custom_call_target="tpu_custom_call" | custom-call | flops 3221225472 | bytes 8912896 | tf_op jit(solution)/shard_map/pallas_call | solution.py:267
  421.0 24.5 %collective-permute-done.38 = bf16[2,192,2048]{2,1,0:T(8,128)(2,1)} collective-permute-done((bf16[2,192,2048]{2,1,0:T(8,128)(2,1)}, bf16[2,192,2048]{2,1,0:T(8,128)(2,1)}, u32[]{:S(2)}, u32[]{:S(2)}) %collective-permute-start.38) | collective-permute-done | bytes 1572896 | tf_op jit(solution)/shard_map/ppermute | solution.py:49
  464.4 8.8 %collective-permute-done.40 = bf16[192,2048]{1,0:T(8,128)(2,1)} collective-permute-done((bf16[192,2048]{1,0:T(8,128)(2,1)}, bf16[192,2048]{1,0:T(8,128)(2,1)}, u32[]{:S(2)}, u32[]{:S(2)}) %collective-permute-start.40) | collective-permute-done | bytes 786464 | tf_op jit(solution)/shard_map/ppermute | solution.py:49
  475.1 7.8 %collective-permute-done.33 = bf16[192,2048]{1,0:T(8,128)(2,1)} collective-permute-done((bf16[192,2048]{1,0:T(8,128)(2,1)}, bf16[192,2048]{1,0:T(8,128)(2,1)}, u32[]{:S(2)}, u32[]{:S(2)}) %collective-permute-start.33) | collective-permute-done | bytes 786464 | tf_op jit(solution)/shard_map/ppermute | solution.py:49
  (205 shorter events, 175.1 us)
Async XLA Ops:
  33.5 103.5 %collective-permute-start = (bf16[768,2048]{1,0:T(8,128)(2,1)}, bf16[768,2048]{1,0:T(8,128)(2,1)}, u32[]{:S(2)}, u32[]{:S(2)}) collective-permute-start(bf16[768,2048]{1,0:T(8,128)(2,1)} %constant_dynamic-slice_fusion.2), channel_id=1, source_target_pairs={{1,8},{3,10},{5,12},{7,14},{8,1},{10,3},{12,5},{14,7},{17,24},{19,... | collective-permute-start | bytes 9437192 | tf_op jit(solution)/shard_map/ppermute | solution.py:40
  37.1 53.6 %collective-permute-start.18 = (f32[30,1024]{0,1:T(8,128)}, f32[30,1024]{0,1:T(8,128)}, u32[]{:S(2)}, u32[]{:S(2)}) collective-permute-start(f32[30,1024]{0,1:T(8,128)} %copy.30), channel_id=1, source_target_pairs={{0,1},{2,3},{4,5},{6,7},{9,8},{11,10},{13,12},{15,14},{16,17},{18,... | collective-permute-start | bytes 368648 | tf_op jit(solution)/shard_map/ppermute | solution.py:49
  51.2 41.9 %collective-permute-start.10 = (bf16[1024,512]{1,0:T(8,128)(2,1)S(1)}, bf16[1024,512]{1,0:T(8,128)(2,1)}, u32[]{:S(2)}, u32[]{:S(2)}) collective-permute-start(bf16[1024,512]{1,0:T(8,128)(2,1)S(1)} %bitcast.128), channel_id=1, source_target_pairs={{1,8},{3,10},{5,12},{7,14},{8,1},{10,3},{12,5},{14,7},{17,24},{19,... | collective-permute-start | bytes 3145736 | tf_op jit(solution)/shard_map/ppermute | solution.py:40
  56.3 37.0 %collective-permute-start.8 = (bf16[2,512,512]{2,1,0:T(8,128)(2,1)}, bf16[2,512,512]{2,1,0:T(8,128)(2,1)}, u32[]{:S(2)}, u32[]{:S(2)}) collective-permute-start(bf16[2,512,512]{2,1,0:T(8,128)(2,1)} %pad_maximum_fusion.11), channel_id=1, source_target_pairs={{0,4},{8,12},{2,6},{10,14},{4,0},{12,8},{6,2},{14,10},{1,5},{9,13}... | collective-permute-start | bytes 3145736 | tf_op jit(solution)/shard_map/ppermute | solution.py:49
  59.7 92.1 %collective-permute-start.21 = (bf16[4,512,512]{2,1,0:T(8,128)(2,1)}, bf16[4,512,512]{2,1,0:T(8,128)(2,1)}, u32[]{:S(2)}, u32[]{:S(2)}) collective-permute-start(bf16[4,512,512]{2,1,0:T(8,128)(2,1)} %pad_maximum_fusion.4.refs_0_), channel_id=1, source_target_pairs={{0,1},{8,9},{2,3},{10,11},{4,5},{12,13},{6,7},{14,15},{1,0},{9,8},... | collective-permute-start | bytes 6291464 | tf_op jit(solution)/shard_map/ppermute | solution.py:49
  93.0 37.0 %collective-permute-start.5 = (bf16[512,512]{1,0:T(8,128)(2,1)S(1)}, bf16[512,512]{1,0:T(8,128)(2,1)S(1)}, u32[]{:S(2)}, u32[]{:S(2)}) collective-permute-start(bf16[512,512]{1,0:T(8,128)(2,1)S(1)} %get-tuple-element.17), channel_id=1, source_target_pairs={{0,16},{1,24},{2,18},{3,26},{4,20},{5,28},{6,22},{7,30},{8,17},{9,... | collective-permute-start | bytes 1572872 | tf_op jit(solution)/shard_map/ppermute | solution.py:40
  93.3 42.5 %collective-permute-start.9 = (bf16[512,512]{1,0:T(8,128)(2,1)S(1)}, bf16[512,512]{1,0:T(8,128)(2,1)S(1)}, u32[]{:S(2)}, u32[]{:S(2)}) collective-permute-start(bf16[512,512]{1,0:T(8,128)(2,1)S(1)} %get-tuple-element.19), channel_id=1, source_target_pairs={{0,16},{1,24},{2,18},{3,26},{4,20},{5,28},{6,22},{7,30},{8,17},{9,... | collective-permute-start | bytes 1572872 | tf_op jit(solution)/shard_map/ppermute | solution.py:40
  134.8 38.8 %collective-permute-start.12 = (bf16[4,512,512]{2,1,0:T(8,128)(2,1)S(1)}, bf16[4,512,512]{2,1,0:T(8,128)(2,1)S(1)}, u32[]{:S(2)}, u32[]{:S(2)}) collective-permute-start(bf16[4,512,512]{2,1,0:T(8,128)(2,1)S(1)} %pad_maximum_fusion.1.refs_0_), channel_id=1, source_target_pairs={{0,1},{8,9},{2,3},{10,11},{4,5},{12,13},{6,7},{14,15},{1,0},{9,8},... | collective-permute-start | bytes 6291464 | tf_op jit(solution)/shard_map/ppermute | solution.py:49
  136.0 31.5 %collective-permute-start.11 = (bf16[2,512,512]{2,1,0:T(8,128)(2,1)S(1)}, bf16[2,512,512]{2,1,0:T(8,128)(2,1)S(1)}, u32[]{:S(2)}, u32[]{:S(2)}) collective-permute-start(bf16[2,512,512]{2,1,0:T(8,128)(2,1)S(1)} %pad_maximum_fusion.12), channel_id=1, source_target_pairs={{0,4},{8,12},{2,6},{10,14},{4,0},{12,8},{6,2},{14,10},{1,5},{9,13}... | collective-permute-start | bytes 3145736 | tf_op jit(solution)/shard_map/ppermute | solution.py:49
  137.0 64.9 %collective-permute-start.1 = (bf16[768,2048]{1,0:T(8,128)(2,1)}, bf16[768,2048]{1,0:T(8,128)(2,1)}, u32[]{:S(2)}, u32[]{:S(2)}) collective-permute-start(bf16[768,2048]{1,0:T(8,128)(2,1)} %collective-permute-done.refs_0_), channel_id=1, source_target_pairs={{8,10},{10,8},{12,14},{14,12},{1,3},{3,1},{5,7},{7,5},{24,26},{26,... | collective-permute-start | bytes 9437192 | tf_op jit(solution)/shard_map/ppermute | solution.py:49
  169.0 44.1 %collective-permute-start.17 = (bf16[4,512,512]{2,1,0:T(8,128)(2,1)}, bf16[4,512,512]{2,1,0:T(8,128)(2,1)}, u32[]{:S(2)}, u32[]{:S(2)}) collective-permute-start(bf16[4,512,512]{2,1,0:T(8,128)(2,1)} %pad_maximum_fusion.3.refs_0_), channel_id=1, source_target_pairs={{0,1},{8,9},{2,3},{10,11},{4,5},{12,13},{6,7},{14,15},{1,0},{9,8},... | collective-permute-start | bytes 6291464 | tf_op jit(solution)/shard_map/ppermute | solution.py:49
  173.7 65.0 %collective-permute-start.26 = (bf16[4,512,512]{2,1,0:T(8,128)(2,1)}, bf16[4,512,512]{2,1,0:T(8,128)(2,1)}, u32[]{:S(2)}, u32[]{:S(2)}) collective-permute-start(bf16[4,512,512]{2,1,0:T(8,128)(2,1)} %pad_maximum_fusion.6.refs_0_), channel_id=1, source_target_pairs={{0,1},{8,9},{2,3},{10,11},{4,5},{12,13},{6,7},{14,15},{1,0},{9,8},... | collective-permute-start | bytes 6291464 | tf_op jit(solution)/shard_map/ppermute | solution.py:49
  199.5 58.9 %collective-permute-start.14 = (bf16[2,512,512]{2,1,0:T(8,128)(2,1)S(1)}, bf16[2,512,512]{2,1,0:T(8,128)(2,1)}, u32[]{:S(2)}, u32[]{:S(2)}) collective-permute-start(bf16[2,512,512]{2,1,0:T(8,128)(2,1)S(1)} %pad_maximum_fusion.13), channel_id=1, source_target_pairs={{0,4},{8,12},{2,6},{10,14},{4,0},{12,8},{6,2},{14,10},{1,5},{9,13}... | collective-permute-start | bytes 3145736 | tf_op jit(solution)/shard_map/ppermute | solution.py:49
  200.6 48.0 %collective-permute-start.23 = (bf16[2,512,512]{2,1,0:T(8,128)(2,1)S(1)}, bf16[2,512,512]{2,1,0:T(8,128)(2,1)S(1)}, u32[]{:S(2)}, u32[]{:S(2)}) collective-permute-start(bf16[2,512,512]{2,1,0:T(8,128)(2,1)S(1)} %pad_maximum_fusion.15), channel_id=1, source_target_pairs={{0,4},{8,12},{2,6},{10,14},{4,0},{12,8},{6,2},{14,10},{1,5},{9,13}... | collective-permute-start | bytes 3145736 | tf_op jit(solution)/shard_map/ppermute | solution.py:49
  235.8 76.6 %collective-permute-start.19 = (bf16[144,512]{0,1:T(8,128)(2,1)}, bf16[144,512]{0,1:T(8,128)(2,1)S(1)}, u32[]{:S(2)}, u32[]{:S(2)}) collective-permute-start(bf16[144,512]{0,1:T(8,128)(2,1)} %pad_maximum_fusion.18), channel_id=1, source_target_pairs={{0,4},{8,12},{2,6},{10,14},{4,1},{12,9},{6,3},{14,11},{1,5},{9,13}... | collective-permute-start | bytes 442376 | tf_op jit(solution)/shard_map/ppermute | solution.py:49
  248.6 31.5 %collective-permute-start.35 = (bf16[1024,256]{1,0:T(8,128)(2,1)}, bf16[1024,256]{1,0:T(8,128)(2,1)S(1)}, u32[]{:S(2)}, u32[]{:S(2)}) collective-permute-start(bf16[1024,256]{1,0:T(8,128)(2,1)} %get-tuple-element.24), channel_id=1, source_target_pairs={{0,16},{1,24},{2,18},{3,26},{4,20},{5,28},{6,22},{7,30},{8,17},{9,... | collective-permute-start | bytes 1572872 | tf_op jit(solution)/shard_map/ppermute | solution.py:40
  258.5 32.8 %collective-permute-start.29 = (bf16[1024,256]{1,0:T(8,128)(2,1)S(1)}, bf16[1024,256]{1,0:T(8,128)(2,1)S(1)}, u32[]{:S(2)}, u32[]{:S(2)}) collective-permute-start(bf16[1024,256]{1,0:T(8,128)(2,1)S(1)} %get-tuple-element.23), channel_id=1, source_target_pairs={{0,16},{1,24},{2,18},{3,26},{4,20},{5,28},{6,22},{7,30},{8,17},{9,... | collective-permute-start | bytes 1572872 | tf_op jit(solution)/shard_map/ppermute | solution.py:40
  287.2 52.8 %collective-permute-start.15 = (bf16[4,512,512]{2,1,0:T(8,128)(2,1)S(1)}, bf16[4,512,512]{2,1,0:T(8,128)(2,1)}, u32[]{:S(2)}, u32[]{:S(2)}) collective-permute-start(bf16[4,512,512]{2,1,0:T(8,128)(2,1)S(1)} %pad_maximum_fusion.2.refs_0_), channel_id=1, source_target_pairs={{0,1},{8,9},{2,3},{10,11},{4,5},{12,13},{6,7},{14,15},{1,0},{9,8},... | collective-permute-start | bytes 6291464 | tf_op jit(solution)/shard_map/ppermute | solution.py:49
  288.8 64.5 %collective-permute-start.24 = (bf16[4,512,512]{2,1,0:T(8,128)(2,1)S(1)}, bf16[4,512,512]{2,1,0:T(8,128)(2,1)}, u32[]{:S(2)}, u32[]{:S(2)}) collective-permute-start(bf16[4,512,512]{2,1,0:T(8,128)(2,1)S(1)} %pad_maximum_fusion.5.refs_0_), channel_id=1, source_target_pairs={{0,1},{8,9},{2,3},{10,11},{4,5},{12,13},{6,7},{14,15},{1,0},{9,8},... | collective-permute-start | bytes 6291464 | tf_op jit(solution)/shard_map/ppermute | solution.py:49
  291.3 45.2 %collective-permute-start.30 = (bf16[2,1024,256]{2,1,0:T(8,128)(2,1)S(1)}, bf16[2,1024,256]{2,1,0:T(8,128)(2,1)}, u32[]{:S(2)}, u32[]{:S(2)}) collective-permute-start(bf16[2,1024,256]{2,1,0:T(8,128)(2,1)S(1)} %pad_maximum_fusion.16), channel_id=1, source_target_pairs={{0,4},{8,12},{2,6},{10,14},{4,0},{12,8},{6,2},{14,10},{1,5},{9,13}... | collective-permute-start | bytes 3145736 | tf_op jit(solution)/shard_map/ppermute | solution.py:49
  312.5 72.1 %collective-permute-start.37 = (bf16[4,1024,256]{2,1,0:T(8,128)(2,1)}, bf16[4,1024,256]{2,1,0:T(8,128)(2,1)}, u32[]{:S(2)}, u32[]{:S(2)}) collective-permute-start(bf16[4,1024,256]{2,1,0:T(8,128)(2,1)} %pad_maximum_fusion.8.refs_2_), channel_id=1, source_target_pairs={{0,1},{8,9},{2,3},{10,11},{4,5},{12,13},{6,7},{14,15},{1,0},{9,8},... | collective-permute-start | bytes 6291464 | tf_op jit(solution)/shard_map/ppermute | solution.py:49
  339.4 69.2 %collective-permute-start.31 = (bf16[4,1024,256]{2,1,0:T(8,128)(2,1)}, bf16[4,1024,256]{2,1,0:T(8,128)(2,1)}, u32[]{:S(2)}, u32[]{:S(2)}) collective-permute-start(bf16[4,1024,256]{2,1,0:T(8,128)(2,1)} %pad_maximum_fusion.7.refs_2_), channel_id=1, source_target_pairs={{0,1},{8,9},{2,3},{10,11},{4,5},{12,13},{6,7},{14,15},{1,0},{9,8},... | collective-permute-start | bytes 6291464 | tf_op jit(solution)/shard_map/ppermute | solution.py:49
  398.2 47.2 %collective-permute-start.38 = (bf16[2,192,2048]{2,1,0:T(8,128)(2,1)}, bf16[2,192,2048]{2,1,0:T(8,128)(2,1)}, u32[]{:S(2)}, u32[]{:S(2)}) collective-permute-start(bf16[2,192,2048]{2,1,0:T(8,128)(2,1)} %get-tuple-element.25), channel_id=1, source_target_pairs={{0,1},{8,0},{2,3},{10,2},{4,5},{12,4},{6,7},{14,6},{1,9},{9,8},{3,... | collective-permute-start | bytes 4718600 | tf_op jit(solution)/shard_map/ppermute | solution.py:49
  419.7 37.6 %collective-permute-start.32 = (bf16[384,2048]{1,0:T(8,128)(2,1)}, bf16[384,2048]{1,0:T(8,128)(2,1)}, u32[]{:S(2)}, u32[]{:S(2)}) collective-permute-start(bf16[384,2048]{1,0:T(8,128)(2,1)} %constant_dynamic-slice_fusion.1), channel_id=1, source_target_pairs={{0,2},{8,10},{2,0},{10,8},{4,6},{12,14},{6,4},{14,12},{1,3},{9,11}... | collective-permute-start | bytes 4718600 | tf_op jit(solution)/shard_map/ppermute | solution.py:49
  (38 other events, 568.2 us)
